TPU v7x, 512 devices: a whole 4x4x16 slice. The times are simulated.
512 devices in a mesh: seq: 64 (over y, x, z_lo), head: 8 (over z_hi, core).
Axes of the slice: x: 4, y: 4, z: 16 (z_hi: 4, z_lo: 4; z = z_hi * 4 + z_lo), core: 2. Of those that a mesh axis runs over, the one named last changes fastest.
Arguments:
- queries: bfloat16 [16384, 5120], P('seq', 'head'), may hold values from -100 to 100
- keys: bfloat16 [16384, 5120], P('seq', 'head'), may hold values from -12 to 12
- values: bfloat16 [16384, 5120], P('seq', 'head'), may hold values from -6 to 6
- hidden: bfloat16 [16384, 5120], P('seq', 'head'), may hold values from -3 to 3
- cached: bfloat16 [16384, 5120], P('seq', 'head'), may hold values from -6 to 6
- active: int32 [16384], P('seq'), may hold values from 0 to 1, as said below
- w_out: bfloat16 [5120, 5120], P('head', 'seq'), may hold values from -0.078125 to 0.078125
Outputs:
- block_output: bfloat16 [16384, 5120], P('seq', 'head')
Inputs may be any that keep to these rules, and one draw needn't show every extreme that they name: `active`: exactly 704 ones in all; among the 256 tokens of one index of seq at most 32 ones, and that many on some of them.
All inputs are finite; a program needn't handle non-finite values.
Results may differ from a plain program's by a relative error of at most 0.0039.
Values may be sent and summed in bfloat16 or wider, within the bound.
A program may use at most 64 MiB of HBM per device.

v0:
```python
import jax
import jax.numpy as jnp
from jax import lax
from jax.sharding import PartitionSpec as P

HD = 128


def for_sending(value):

    def short(part):
        return part.astype(jnp.bfloat16) if part.dtype == jnp.float32 else part

    return jax.tree.map(short, value)


def local_partials(query_rows, keys, values):
    head_count = keys.shape[1] // HD
    inv_root = 1.0 / HD**0.5

    def one_head(head):
        start = head * HD
        q_head = lax.dynamic_slice_in_dim(query_rows, start, HD, 1)
        k_head = lax.dynamic_slice_in_dim(keys, start, HD, 1)
        v_head = lax.dynamic_slice_in_dim(values, start, HD, 1)
        scores = (
            lax.dot_general(
                q_head, k_head, (((1,), (1,)), ((), ())), preferred_element_type=jnp.float32
            )
            * inv_root
        )
        peak = jnp.max(scores, axis=1)
        expo = jnp.exp(scores - peak[:, None])
        total = jnp.sum(expo, axis=1)
        block_out = jnp.dot(expo.astype(jnp.bfloat16), v_head, preferred_element_type=jnp.float32)
        return ((block_out / total[:, None]).astype(jnp.bfloat16), peak, total)

    return lax.map(one_head, jnp.arange(head_count, dtype=jnp.int32))


def shards(queries, keys, values, hidden, cached, active, w_out):
    tok_dev, features = queries.shape
    head_count = features // HD
    devices = lax.axis_size("seq")
    capacity = tok_dev // 8
    act_rows = jnp.nonzero(active, size=capacity, fill_value=tok_dev)[0].astype(jnp.int32)
    safe_rows = jnp.minimum(act_rows, tok_dev - 1)
    own_queries = queries[safe_rows]
    gathered = lax.all_gather(own_queries, "seq", axis=0, tiled=True)
    block_out, block_peak, block_total = local_partials(gathered, keys, values)
    block_out = block_out.reshape(head_count, devices, capacity, HD)
    peak_in, total_in = (
        lax.all_to_all(
            block_peak.reshape(head_count, devices, capacity),
            "seq",
            split_axis=1,
            concat_axis=1,
            tiled=True,
        ),
        lax.all_to_all(
            block_total.reshape(head_count, devices, capacity),
            "seq",
            split_axis=1,
            concat_axis=1,
            tiled=True,
        ),
    )
    out_in = lax.all_to_all(
        for_sending(block_out), "seq", split_axis=1, concat_axis=1, tiled=True
    ).astype(block_out.dtype)
    top_max = jnp.max(peak_in, axis=1, keepdims=True)
    weight = total_in * jnp.exp(peak_in - top_max)
    mixed = jnp.einsum("hnc,hncd->hcd", weight, out_in.astype(jnp.float32))
    mixed = mixed / jnp.sum(weight, axis=1)[:, :, None]
    attn = jnp.transpose(mixed, (1, 0, 2)).reshape(capacity, features).astype(jnp.bfloat16)
    terms = jnp.dot(
        attn, lax.all_gather(w_out, "seq", axis=1, tiled=True), preferred_element_type=jnp.float32
    )
    summed = lax.psum_scatter(
        terms.astype(jnp.bfloat16), "head", scatter_dimension=1, tiled=True
    ).astype(jnp.float32)
    updated = (hidden[safe_rows].astype(jnp.float32) + summed).astype(jnp.bfloat16)
    return cached.at[act_rows].set(updated, mode="drop")


def solution(mesh):
    placed = (
        P("seq", "head"),
        P("seq", "head"),
        P("seq", "head"),
        P("seq", "head"),
        P("seq", "head"),
        P("seq"),
        P("head", "seq"),
    )
    return jax.shard_map(
        shards, mesh=mesh, in_specs=placed, out_specs=P("seq", "head"), check_vma=False
    )
```

profile of v0, /device:TPU:1, one launch (start us, length us, event | category | flops | bytes accessed | tf_op | source)
XLA Modules:
  0.0 835.7 jit_solution(14401901333159567819)
XLA Ops:
  6.5 1.8 copy.56
  9.0 1.4 fusion.25
  11.0 2.3 scatter_custom_fusion
  13.5 1.3 fusion.23
  14.8 2.3 gather_fusion
  17.9 318.7 %all-gather.6.cloned.1.call-done = bf16[2048,640]{1,0:T(8,128)(2,1)} async-done(((bf16[32,640]{1,0:T(8,128)(2,1)}), bf16[2048,640]{1,0:T(8,128)(2,1)}) %all-gather.6.cloned.1.call-update) | async-done | bytes 2621456 | tf_op jit(solution)/shard_map/all_gather | solution.py:49
  336.5 25.5 %while.14 = (s32[]{:T(128)}, bf16[5,2048,128]{2,1,0:T(8,128)(2,1)S(1)}, f32[5,2048]{1,0:T(8,128)S(1)}, f32[5,2048]{1,0:T(8,128)S(1)}, s32[5]{0:T(128)S(1)}, /*in...) while((s32[]{:T(128)}, ...), condition=%wide.region_8.9_spmd, body=%wide.region_5.8_spmd.sunk | while | flops 272101376 | bytes 7546555 | solution.py:38
  337.8 1.5 fusion.39
  339.6 1.6 fusion.41
  342.9 1.5 fusion.39
  344.7 1.6 fusion.41
  348.0 1.5 fusion.39
  349.8 1.6 fusion.41
  353.1 1.5 fusion.39
  354.9 1.6 fusion.41
  358.2 1.5 fusion.39
  360.0 1.6 fusion.41
  363.0 7.7 all-to-all-start.2
  371.7 7.9 all-to-all-done.2
  379.6 4.6 all-to-all-start.1
  384.2 2.0 copy.16
  386.2 6.8 all-to-all-done.1
  393.0 4.7 all-to-all-start
  400.7 1.4 fusion.16
  403.2 1.4 fusion.15
  405.3 55.5 %all-to-all-done = bf16[5,64,32,128]{3,2,0,1:T(8,128)(2,1)S(1)} async-done(((bf16[5,64,32,128]{3,2,0,1:T(8,128)(2,1)}), bf16[5,64,32,128]{3,2,0,1:T(8,128)(2,1)S(1)}, u32[]{:S(2)}, u32[]{:S(2)}) %all-to-all-start) | async-done | bytes 2621472 | tf_op jit(solution)/shard_map/all_to_all | solution.py:68
  460.8 1.4 fusion.12
  462.3 259.2 %all-gather.4.cloned.1.call-done = bf16[640,5120]{0,1:T(8,128)(2,1)} async-done(((bf16[640,80]{0,1:T(8,128)(2,1)}), bf16[640,5120]{0,1:T(8,128)(2,1)}) %all-gather.4.cloned.1.call-update) | async-done | bytes 6553616 | tf_op jit(solution)/shard_map/all_gather | solution.py:77
  721.5 4.9 convolution_convert_fusion
  726.5 1.4 copy.24
  727.9 97.5 %reduce-scatter.4.cloned.1.call-done = bf16[640,32]{1,0:T(8,128)(2,1)} async-done(((bf16[5120,32]{1,0:T(8,128)(2,1)}), bf16[640,32]{1,0:T(8,128)(2,1)}) %reduce-scatter.4.cloned.1.call-update) | async-done | bytes 40976
  826.5 2.7 scatter_custom_fusion.1
  (63 shorter events, 16.6 us)
Async XLA Ops:
  6.5 819.9 %copy-start = (bf16[256,640]{1,0:T(8,128)(2,1)S(1)}, bf16[256,640]{1,0:T(8,128)(2,1)}, u32[]{:S(2)}) copy-start(bf16[256,640]{1,0:T(8,128)(2,1)} %param.12) | copy-start | bytes 983044
  6.5 330.0 %all-gather.6.cloned.1.call-start = ((), (), s32[]{:S(2)}) async-start(), calls=%async_computation.5 | async-start | bytes 2662400 | tf_op jit(solution)/shard_map/all_gather | solution.py:49
  14.8 2.3 copy-start.1
  17.1 704.4 %all-gather.4.cloned.1.call-start = ((), (), s32[]{:S(2)}) async-start(), calls=%async_computation.4 | async-start | bytes 6656000 | tf_op jit(solution)/shard_map/all_gather | solution.py:77
  363.0 16.5 %all-to-all-start.2 = ((f32[64,1,160]{2,1,0:T(1,128)}), f32[64,1,160]{2,1,0:T(1,128)S(1)}, u32[]{:S(2)}, u32[]{:S(2)}) async-start(f32[64,1,160]{2,1,0:T(1,128)} %reshape.196), calls=%async_computation.2 | async-start | bytes 131072 | tf_op jit(solution)/shard_map/all_to_all | solution.py:53
  379.6 13.5 %all-to-all-start.1 = ((f32[64,1,160]{2,1,0:T(1,128)}), f32[64,1,160]{2,1,0:T(1,128)S(1)}, u32[]{:S(2)}, u32[]{:S(2)}) async-start(f32[64,1,160]{2,1,0:T(1,128)} %reshape.194), calls=%async_computation.1 | async-start | bytes 131072 | tf_op jit(solution)/shard_map/all_to_all | solution.py:60
  393.0 67.8 %all-to-all-start = ((bf16[5,64,32,128]{3,2,0,1:T(8,128)(2,1)}), bf16[5,64,32,128]{3,2,0,1:T(8,128)(2,1)S(1)}, u32[]{:S(2)}, u32[]{:S(2)}) async-start(bf16[5,64,32,128]{3,2,0,1:T(8,128)(2,1)} %copy.16), calls=%async_computation | async-start | bytes 5242880 | tf_op jit(solution)/shard_map/all_to_all | solution.py:68
  397.7 427.7 %reduce-scatter.4.cloned.1.call-start = ((), (), s32[]{:S(2)}) async-start(), calls=%async_computation.6 | async-start | bytes 1474560
  726.4 100.0 %copy-start.2 = (s32[1024]{0:T(1024)S(1)}, s32[1024]{0:T(1024)}, u32[]{:S(2)}) copy-start(s32[1024]{0:T(1024)} %copy-done.1) | copy-start | bytes 12292
Sparse Core Ops, SparseCore 0:
  17.2 319.2 all-gather.5
  338.6 382.8 all-gather.3
  728.0 97.3 reduce-scatter.3
where the time goes:
time: 837 us; the launch traced here: 836 us
  waiting for transfers between devices  746 us (89%)
  matrix products  21.9 us (3%)
  local copies, waits for them, and re-layouts  18.3 us (2%)
  starting transfers between devices  17.1 us (2%)
  other arithmetic  15.5 us (2%)
  between operations  13.3 us (2%)
    all_gather x1, waiting for transfers between devices, shards(): gathered = lax.all_gather(own_queries, 'seq', axis=0, tiled=True)  319 us
    all_gather x1, waiting for transfers between devices, shards(): lax.all_gather(w_out, 'seq', axis=1, tiled=True)  259 us
    unnamed x4, waiting for transfers between devices  98.2 us
    all_to_all x1, waiting for transfers between devices, shards(): lax.all_to_all(for_sending(block_out), 'seq', split_axis=1, concat_axis=1...  55.5 us
  transfers between devices with their start and end apart: 6, of which 6 were waited for; matrix products, arithmetic and copies ran while one was open for 4% of the time, Pallas kernels for 0%

commit v1 on v0

v1 whole, which is shorter than its diff:
```python
import jax
import jax.numpy as jnp
from jax import lax
from jax.experimental import pallas as pl
from jax.experimental.pallas import tpu as pltpu
from jax.sharding import PartitionSpec as P

X, Y, Z, H = 4, 4, 4, 8
HD = 128
CAP = 32
CR = 48
BF = jnp.bfloat16
F32 = jnp.float32
NA, NB = 3, 2
MESH = pl.DeviceIdType.MESH


def log2(n):
    return n.bit_length() - 1


def iota(shape, dim):
    return lax.broadcasted_iota(jnp.int32, shape, dim)


def onehot(cond):
    return jnp.where(cond, 1.0, 0.0).astype(BF)


def mm(a, b):
    return jnp.dot(a, b, preferred_element_type=F32)


def mm_nt(a, b):
    return lax.dot_general(a, b, (((1,), (1,)), ((), ())), preferred_element_type=F32)


def pack_stat(tile):
    lane = iota(tile.shape, 1)
    hi = tile.astype(BF).astype(F32)
    rest = tile - hi
    mid = rest.astype(BF).astype(F32)
    low = rest - mid
    return jnp.where(lane < 8, hi, jnp.where(lane < 16, mid, jnp.where(lane < 24, low, 0.0))).astype(BF)


def merge(sources, heads, sel):
    width = heads * HD
    logs = [mm(s[:, width:], sel[:, :width]) for s in sources]
    top = logs[0]
    for part in logs[1:]:
        top = jnp.maximum(top, part)
    total, mixed = None, None
    for s, part in zip(sources, logs):
        w = jnp.exp(part - top)
        term = w * s[:, :width].astype(F32)
        total = w if total is None else total + w
        mixed = term if mixed is None else mixed + term
    return mixed / total, top + jnp.log(total)


def stat_of(logs, heads):
    lane = iota((logs.shape[0], HD), 1)
    tile = jnp.zeros((logs.shape[0], HD), F32)
    for h in range(heads):
        tile = jnp.where((lane & 7) == h, logs[:, h * HD : (h + 1) * HD], tile)
    return pack_stat(tile)


def body(
    q_ref, k_ref, v_ref, hid_ref, cac_ref, act_ref, w_ref, out_ref,
    qa, qb, cnt, wt, qc, sel, rsel, expand,
    pa, pb, ra, rb, a2, b2, ra2, rb2, a3, b3, ra3, rb3,
    ht, hr, fin, zs, zr, send_sem, recv_sem,
):
    tok, feat = q_ref.shape
    wc = w_ref.shape[1]
    half = NA * HD
    bs_a, bs_b = Y * Z * 16, X * Z * 16
    nr = Y * X * CR
    me, h = lax.axis_index("seq"), lax.axis_index("head")
    z = me & (Z - 1)
    x = (me >> log2(Z)) & (X - 1)
    y = me >> log2(Z * X)

    def xp(d):
        return (y * X + ((x + d) & (X - 1))) * Z + z, h

    def yp(d):
        return (((y + d) & (Y - 1)) * X + x) * Z + z, h

    def zp(d):
        return (y * X + x) * Z + ((z + d) & (Z - 1)), h

    def hp(d):
        return me, (h + d) & (H - 1)

    barrier = pltpu.get_barrier_semaphore()
    peers = (
        [xp(d) for d in range(1, X)] + [yp(d) for d in range(1, Y)] + [zp(d) for d in range(1, Z)] + [hp(d) for d in range(1, H)]
    )
    for p in peers:
        pl.semaphore_signal(barrier, inc=1, device_id=p, device_id_type=MESH)

    counter = [0]

    def copies(make, peer, n):
        found = []
        for d in range(1, n):
            i = counter[0]
            counter[0] += 1
            src, dst = make(d)
            found.append(
                pltpu.make_async_remote_copy(
                    src_ref=src, dst_ref=dst, send_sem=send_sem.at[i], recv_sem=recv_sem.at[i],
                    device_id=peer(d), device_id_type=MESH,
                )
            )
        return found

    every = []

    def start(cs):
        for c in cs:
            c.start()
        every.extend(cs)

    def arrive(cs):
        for c in cs:
            c.wait_recv()

    act = act_ref[...]
    act8 = jnp.broadcast_to(act, (8, tok)).astype(F32).astype(BF)
    before = onehot(iota((tok, tok), 0) < iota((tok, tok), 1))
    rank = mm(act8, before)[0:1, :]
    pick = onehot((iota((CAP, tok), 0).astype(F32) == rank) & (act > 0))
    own = mm(pick, q_ref[...]).astype(BF)
    qa[x, y, z] = own[0:16]
    qb[y, x, z] = own[16:32]
    total = jnp.sum(act.astype(F32), axis=1, keepdims=True)
    cnt[x, y, z] = jnp.where(iota((1, HD), 1) == me, total, 0.0)
    eye = onehot(iota((wc, wc), 0) == iota((wc, wc), 1))
    wt[y, x] = mm_nt(eye, w_ref[...]).astype(BF)

    pl.semaphore_wait(barrier, len(peers))

    cz = copies(lambda d: (cnt.at[x, y, z],) * 2, zp, Z)
    az = copies(lambda d: (qa.at[x, y, z],) * 2, zp, Z)
    bz = copies(lambda d: (qb.at[y, x, z],) * 2, zp, Z)
    start(cz)
    start(az)
    start(bz)
    w0 = pl.ds(0, half)
    w1 = pl.ds(half, feat - half)
    wx0 = copies(lambda d: (wt.at[y, x, :, w0],) * 2, xp, X)
    wy1 = copies(lambda d: (wt.at[y, x, :, w1],) * 2, yp, Y)
    start(wx0)
    start(wy1)

    expand[...] = mm_nt(onehot(iota((tok, tok), 0) == iota((tok, tok), 1)), pick).astype(BF)
    lane, col = iota((HD, half), 0), iota((HD, half), 1)
    sel[...] = onehot(((lane & 7) == (col >> log2(HD))) & (lane < 24))
    ht[...] = jnp.zeros_like(ht)

    cy = copies(lambda d: (cnt.at[x, y],) * 2, yp, Y)
    ay = copies(lambda d: (qa.at[x, y],) * 2, yp, Y)
    bx = copies(lambda d: (qb.at[y, x],) * 2, xp, X)
    arrive(cz)
    start(cy)
    arrive(az)
    start(ay)
    arrive(bz)
    start(bx)
    cx = copies(lambda d: (cnt.at[x],) * 2, xp, X)
    ax = copies(lambda d: (qa.at[x],) * 2, xp, X)
    by = copies(lambda d: (qb.at[y],) * 2, yp, Y)
    arrive(cy)
    start(cx)
    arrive(ay)
    start(ax)
    arrive(bx)
    start(by)
    arrive(cx)

    counts = jnp.sum(cnt[...].reshape(X * Y * Z, HD), axis=0, keepdims=True)
    cnt8 = jnp.broadcast_to(counts, (8, HD)).astype(BF)

    def positions(part, block, size):
        j = iota((HD, size), 1)
        zz = (j >> 4) & (Z - 1)
        o = j >> (4 + log2(Z))
        s = ((o * X + block) if part == 0 else (block * X + o)) * Z + zz
        b = iota((HD, size), 0)
        off = mm(cnt8, onehot(b < s))[0:1, :]
        n = mm(cnt8, onehot(b == s))[0:1, :]
        r = ((j[0:1, :] & 15) + 16 * part).astype(F32)
        return jnp.where(r < n, off + r, -1.0)

    def compact(part, block, size, rows, first):
        pos = positions(part, block, size)

        @pl.loop(0, Y)
        def _(yb):
            i = iota((X * CR, size), 0) + yb * (X * CR)
            got = mm(onehot(i.astype(F32) == pos), rows).astype(BF)
            qc[yb] = got if first else qc[yb] + got

    compact(0, x, bs_a, qa[x].reshape(bs_a, feat), True)
    compact(1, y, bs_b, qb[y].reshape(bs_b, feat), False)
    slot, b = iota((Z * CAP, HD), 0), iota((Z * CAP, HD), 1)
    off = mm_nt(onehot(b < (y * X + x) * Z + (slot >> log2(CAP))), cnt8)[:, 0:1]
    want = off + (slot[:, 0:1] & (CAP - 1)).astype(F32)
    rsel[...] = onehot(iota((Z * CAP, nr), 1).astype(F32) == want)

    for d in range(1, max(X, Y)):
        if d < X:
            arrive(ax[d - 1 : d])
            xb = (x - d) & (X - 1)
            compact(0, xb, bs_a, qa[xb].reshape(bs_a, feat), False)
        if d < Y:
            arrive(by[d - 1 : d])
            yb = (y - d) & (Y - 1)
            compact(1, yb, bs_b, qb[yb].reshape(bs_b, feat), False)

    wy0 = copies(lambda d: (wt.at[y, :, :, w0],) * 2, yp, Y)
    wx1 = copies(lambda d: (wt.at[:, x, :, w1],) * 2, xp, X)
    arrive(wx0)
    start(wy0)
    arrive(wy1)
    start(wx1)

    scale = 1.0 / HD**0.5

    def attend(first, heads, dest):
        @pl.loop(0, Y)
        def _(yb):
            lane = iota((X * CR, HD), 1)
            tile = jnp.zeros((X * CR, HD), F32)
            for i in range(heads):
                c = slice((first + i) * HD, (first + i + 1) * HD)
                score = mm_nt(qc[yb, :, c], k_ref[:, c]) * scale
                peak = jnp.max(score, axis=1, keepdims=True)
                expo = jnp.exp(score - peak)
                total = jnp.sum(expo, axis=1, keepdims=True)
                part = mm(expo.astype(BF), v_ref[:, c]) / total
                dest[yb, :, :, i * HD : (i + 1) * HD] = part.astype(BF).reshape(X, CR, HD)
                tile = jnp.where((lane & 7) == i, peak + jnp.log(total), tile)
            dest[yb, :, :, heads * HD :] = pack_stat(tile).reshape(X, CR, HD)

    attend(0, NA, pa)
    sa = copies(lambda d: (pa.at[(y + d) & (Y - 1)], ra.at[d - 1]), yp, Y)
    start(sa)
    attend(NA, NB, pb)
    sb = copies(lambda d: (pb.at[:, (x + d) & (X - 1)], rb.at[d - 1]), xp, X)
    start(sb)

    arrive(sa)

    @pl.loop(0, X)
    def _(i):
        mean, logs = merge([pa[y, i]] + [ra[d, i] for d in range(Y - 1)], NA, sel[...])
        a2[i, :, :half] = mean.astype(BF)
        a2[i, :, half:] = stat_of(logs, NA)

    sa2 = copies(lambda d: (a2.at[(x + d) & (X - 1)], ra2.at[d - 1]), xp, X)
    start(sa2)
    arrive(sb)

    @pl.loop(0, Y)
    def _(i):
        mean, logs = merge([pb[i, x]] + [rb[d, i] for d in range(X - 1)], NB, sel[...])
        b2[i, :, : NB * HD] = mean.astype(BF)
        b2[i, :, NB * HD :] = stat_of(logs, NB)

    sb2 = copies(lambda d: (b2.at[(y + d) & (Y - 1)], rb2.at[d - 1]), yp, Y)
    start(sb2)
    arrive(sa2)
    mean, logs = merge([a2[x]] + [ra2[d] for d in range(X - 1)], NA, sel[...])
    a3[:, :half] = mean.astype(BF)
    a3[:, half:] = stat_of(logs, NA)
    sa3 = copies(lambda d: (a3, ra3.at[d - 1]), zp, Z)
    start(sa3)
    arrive(sb2)
    mean, logs = merge([b2[y]] + [rb2[d] for d in range(Y - 1)], NB, sel[...])
    b3[:, : NB * HD] = mean.astype(BF)
    b3[:, NB * HD :] = stat_of(logs, NB)
    sb3 = copies(lambda d: (b3, rb3.at[d - 1]), zp, Z)
    start(sb3)
    arrive(sa3)
    attn_a = merge([a3[...]] + [ra3[d] for d in range(Z - 1)], NA, sel[...])[0].astype(BF)
    arrive(wy0)
    arrive(wx1)
    arrive(sb3)
    attn_b = merge([b3[...]] + [rb3[d] for d in range(Z - 1)], NB, sel[...])[0].astype(BF)

    pieces = X * Y // H
    for o in range(H):
        yy, xx = o * pieces // X, o * pieces % X
        w_o = wt[yy, xx : xx + pieces].reshape(pieces * wc, feat)
        term = mm_nt(attn_a, w_o[:, :half]) + mm_nt(attn_b, w_o[:, half:])
        ht[o, :, : pieces * wc] = term.astype(BF)
    sh = copies(lambda d: (ht.at[(h + d) & (H - 1)], hr.at[d - 1]), hp, H)
    start(sh)
    proj = ht[h].astype(F32)
    for d in range(1, H):
        arrive(sh[d - 1 : d])
        proj = proj + hr[d - 1].astype(F32)
    fin[y, x] = proj.astype(BF)

    fx = copies(lambda d: (fin.at[y, x],) * 2, xp, X)
    start(fx)
    arrive(fx)
    fy = copies(lambda d: (fin.at[y],) * 2, yp, Y)
    start(fy)
    arrive(fy)
    zs[...] = mm(rsel[...], fin[...].reshape(nr, 2 * HD)).astype(BF).reshape(Z, CAP, 2 * HD)
    sz = copies(lambda d: (zs.at[(z + d) & (Z - 1)], zr.at[d - 1]), zp, Z)
    start(sz)

    def place(rows, zz):
        l, c = iota((2 * HD, feat), 0), iota((2 * HD, feat), 1)
        second = l >= wc
        at = jnp.where(second, Z * wc - wc, 0) + zz * wc + l
        return mm(rows, onehot((c == at) & (l < pieces * wc)))

    rows = place(zs[z], z)
    for d in range(1, Z):
        arrive(sz[d - 1 : d])
        rows = rows + place(zr[d - 1], (z - d) & (Z - 1))
    grown = mm(expand[...], rows.astype(BF))
    live = mm(expand[...], jnp.ones((CAP, feat), BF)) > 0.5
    out_ref[...] = jnp.where(live, hid_ref[...].astype(F32) + grown, cac_ref[...].astype(F32)).astype(BF)
    for c in every:
        c.wait_send()


def shards(queries, keys, values, hidden, cached, active, w_out):
    tok, feat = queries.shape
    wc = w_out.shape[1]
    wa, wb = (NA + 1) * HD, (NB + 1) * HD
    n_copies = 3 * (Z - 1) + 5 * (X - 1) + 5 * (Y - 1) + 2 * (X + Y - 2) + 3 * (Z - 1) + (H - 1) + 3 * (X + Y)
    vmem = pltpu.VMEM
    scratch = [
        vmem((X, Y, Z, 16, feat), BF),
        vmem((Y, X, Z, 16, feat), BF),
        vmem((X, Y, Z, 1, HD), F32),
        vmem((Y, X, wc, feat), BF),
        vmem((Y, X * CR, feat), BF),
        vmem((HD, NA * HD), BF),
        vmem((Z * CAP, Y * X * CR), BF),
        vmem((tok, CAP), BF),
        vmem((Y, X, CR, wa), BF),
        vmem((Y, X, CR, wb), BF),
        vmem((Y - 1, X, CR, wa), BF),
        vmem((X - 1, Y, CR, wb), BF),
        vmem((X, CR, wa), BF),
        vmem((Y, CR, wb), BF),
        vmem((X - 1, CR, wa), BF),
        vmem((Y - 1, CR, wb), BF),
        vmem((CR, wa), BF),
        vmem((CR, wb), BF),
        vmem((Z - 1, CR, wa), BF),
        vmem((Z - 1, CR, wb), BF),
        vmem((H, CR, 2 * HD), BF),
        vmem((H - 1, CR, 2 * HD), BF),
        vmem((Y, X, CR, 2 * HD), BF),
        vmem((Z, CAP, 2 * HD), BF),
        vmem((Z - 1, CAP, 2 * HD), BF),
        pltpu.SemaphoreType.DMA((n_copies,)),
        pltpu.SemaphoreType.DMA((n_copies,)),
    ]
    return pl.pallas_call(
        body,
        out_shape=jax.ShapeDtypeStruct((tok, feat), BF),
        in_specs=[pl.BlockSpec(memory_space=pltpu.VMEM)] * 7,
        out_specs=pl.BlockSpec(memory_space=pltpu.VMEM),
        scratch_shapes=scratch,
        compiler_params=pltpu.CompilerParams(
            collective_id=0, has_side_effects=True, vmem_limit_bytes=48 * 2**20
        ),
    )(queries, keys, values, hidden, cached, active.reshape(1, tok), w_out)


def solution(mesh):
    placed = (
        P("seq", "head"),
        P("seq", "head"),
        P("seq", "head"),
        P("seq", "head"),
        P("seq", "head"),
        P("seq"),
        P("head", "seq"),
    )
    return jax.shard_map(
        shards, mesh=mesh, in_specs=placed, out_specs=P("seq", "head"), check_vma=False
    )
```

time: 837 us -> 113 us (0.14)
  waiting for transfers between devices: 746 us -> 0 us
  Pallas kernels: 0 us -> 106 us
  matrix products: 21.9 us -> 0 us
  starting transfers between devices: 17.1 us -> 0 us
  other arithmetic: 15.5 us -> 0 us
  between operations: 13.3 us -> 0.03 us
  local copies, waits for them, and re-layouts: 18.3 us -> 6.66 us
    all_gather x2 -> x0, waiting for transfers between devices: 578 us -> none  [the longest x1 319 us: shards(): gathered = lax.all_gather(own_queries, 'seq', axis=0, tiled=True)]
    pallas_call x0 -> x1, Pallas kernels: none -> 106 us  [shards(): pl.pallas_call(body, out_shape=jax.ShapeDtypeStruct((tok, feat), BF), in_...]
    unnamed x4 -> x0, waiting for transfers between devices: 98.2 us -> none
    all_to_all x3 -> x0, waiting for transfers between devices: 70.2 us -> none  [the longest x1 55.5 us: shards(): lax.all_to_all(for_sending(block_out), 'seq', split_axis=1, concat_axis=1...]
    dot_general x12 -> x0, matrix products: 21.9 us -> none  [the longest x5 8.14 us: one_head(): jnp.dot(expo.astype(jnp.bfloat16), v_head, preferred_element_type=jnp.flo...]
    all_to_all x3 -> x0, starting transfers between devices: 17 us -> none  [the longest x1 7.68 us: shards(): lax.all_to_all(block_peak.reshape(head_count, devices, capacity), 'seq',...]
  transfers between devices with their start and end apart: 6 -> 0, of which waited for: 6 -> 0; matrix products, arithmetic and copies ran while one was open for 4% -> 0% of each run, Pallas kernels for 0% -> 0%
where the time goes in v1:
time: 113 us
  Pallas kernels  106 us (94%)
  local copies, waits for them, and re-layouts  6.66 us (6%)
    pallas_call x1, Pallas kernels, shards(): pl.pallas_call(body, out_shape=jax.ShapeDtypeStruct((tok, feat), BF), in_...  106 us
    unnamed x14, local copies, waits for them, and re-layouts  6.66 us

profile of v1, /device:TPU:1, one launch (start us, length us, event | category | flops | bytes accessed | tf_op | source)
XLA Modules:
  0.0 113.2 jit_solution(11940405400434050182)
XLA Ops:
  0.0 0.0 copy-start.5
  0.0 1.1 copy.8.w_ref
  1.1 0.0 copy-done.5
  1.1 0.0 copy-start
  1.1 1.0 copy-done
  2.1 0.0 copy-start.1
  2.1 1.0 copy-done.1
  3.0 0.0 copy-start.2
  3.0 1.0 copy-done.2
  4.0 0.0 copy-start.3
  4.0 1.0 copy-done.3
  5.0 0.0 copy-start.4
  5.0 1.0 copy-done.4
  5.9 106.5 %shard_map.73 = bf16[256,640]{1,0:T(8,128)(2,1)S(1)} custom-call(bf16[256,640]{1,0:T(8,128)(2,1)S(1)} %copy-done, bf16[256,640]{1,0:T(8,128)(2,1)S(1)} %copy-done.1, bf16[256,640]{1,0:T(8,128)(2,1)S(1)} %copy-done.2, bf16[256,640]{1,0:T(8,128)(2,1)S(1)} %copy-done.3, bf16[256,640]{1,0:T(8,128)(2,1)S(1)} %copy-done.4, s32[1,256]{1,0:T(1,128)S(1)} %bitcast.1, ...), custom_call_target="tpu_custom_call" | custom-call | tf_op jit(solution)/shard_map/pallas_call | solution.py:372
  112.4 0.7 copy.10
Async XLA Ops:
  0.0 1.1 copy-start.5
  1.1 1.0 copy-start
  2.1 1.0 copy-start.1
  3.0 1.0 copy-start.2
  4.0 1.0 copy-start.3
  5.0 1.0 copy-start.4

commit v2 on v1

--- a/solution.py
+++ b/solution.py
@@ -1,3 +1,5 @@
+import math
+
 import jax
 import jax.numpy as jnp
 from jax import lax
@@ -27,6 +29,10 @@
     return jnp.where(cond, 1.0, 0.0).astype(BF)
 
 
+def log2_of(v):
+    return jnp.log(v) * (1.0 / math.log(2.0))
+
+
 def mm(a, b):
     return jnp.dot(a, b, preferred_element_type=F32)
 
@@ -52,11 +58,11 @@
         top = jnp.maximum(top, part)
     total, mixed = None, None
     for s, part in zip(sources, logs):
-        w = jnp.exp(part - top)
+        w = lax.exp2(part - top)
         term = w * s[:, :width].astype(F32)
         total = w if total is None else total + w
         mixed = term if mixed is None else mixed + term
-    return mixed / total, top + jnp.log(total)
+    return mixed / total, top + log2_of(total)
 
 
 def stat_of(logs, heads):
@@ -68,15 +74,15 @@
 
 
 def body(
-    q_ref, k_ref, v_ref, hid_ref, cac_ref, act_ref, w_ref, out_ref,
-    qa, qb, cnt, wt, qc, sel, rsel, expand,
+    q_hbm, k_hbm, v_hbm, hid_hbm, cac_hbm, act_hbm, w_hbm, out_ref,
+    q_ref, k_ref, v_ref, hid_ref, cac_ref, act_ref,
+    qa, qb, cnt, wt, pma, pmb, vx, sel, rsel, expand,
     pa, pb, ra, rb, a2, b2, ra2, rb2, a3, b3, ra3, rb3,
-    ht, hr, fin, zs, zr, send_sem, recv_sem,
+    ht, hr, fin, zs, zr, send_sem, recv_sem, load_sem,
 ):
     tok, feat = q_ref.shape
-    wc = w_ref.shape[1]
+    wc = w_hbm.shape[0]
     half = NA * HD
-    bs_a, bs_b = Y * Z * 16, X * Z * 16
     nr = Y * X * CR
     me, h = lax.axis_index("seq"), lax.axis_index("head")
     z = me & (Z - 1)
@@ -102,11 +108,24 @@
     for p in peers:
         pl.semaphore_signal(barrier, inc=1, device_id=p, device_id_type=MESH)
 
+    loads = [
+        pltpu.make_async_copy(src, dst, load_sem.at[i])
+        for i, (src, dst) in enumerate(
+            [
+                (act_hbm, act_ref), (q_hbm, q_ref), (w_hbm, wt.at[y, x]),
+                (k_hbm, k_ref), (v_hbm, v_ref), (hid_hbm, hid_ref), (cac_hbm, cac_ref),
+            ]
+        )
+    ]
+    for c in loads:
+        c.start()
+
     counter = [0]
-
-    def copies(make, peer, n):
+    every = []
+
+    def copies(make, peer, n, steps=None):
         found = []
-        for d in range(1, n):
+        for d in range(1, n) if steps is None else steps:
             i = counter[0]
             counter[0] += 1
             src, dst = make(d)
@@ -118,8 +137,6 @@
             )
         return found
 
-    every = []
-
     def start(cs):
         for c in cs:
             c.start()
@@ -129,24 +146,34 @@
         for c in cs:
             c.wait_recv()
 
+    def ring(block, peer, n, at):
+        direct = copies(lambda d: (block(at, 0, Z),) * 2, peer, n, [1, n - 1] if n > 2 else [1] * (n - 1))
+        on = []
+        if n > 2:
+            on += copies(lambda d: (block((at - 1) & (n - 1), 0, Z // 2),) * 2, peer, n, [1])
+            on += copies(lambda d: (block((at + 1) & (n - 1), Z // 2, Z),) * 2, peer, n, [n - 1])
+        return direct, on
+
+    loads[0].wait()
     act = act_ref[...]
     act8 = jnp.broadcast_to(act, (8, tok)).astype(F32).astype(BF)
     before = onehot(iota((tok, tok), 0) < iota((tok, tok), 1))
     rank = mm(act8, before)[0:1, :]
     pick = onehot((iota((CAP, tok), 0).astype(F32) == rank) & (act > 0))
-    own = mm(pick, q_ref[...]).astype(BF)
-    qa[x, y, z] = own[0:16]
-    qb[y, x, z] = own[16:32]
     total = jnp.sum(act.astype(F32), axis=1, keepdims=True)
     cnt[x, y, z] = jnp.where(iota((1, HD), 1) == me, total, 0.0)
-    eye = onehot(iota((wc, wc), 0) == iota((wc, wc), 1))
-    wt[y, x] = mm_nt(eye, w_ref[...]).astype(BF)
+    loads[1].wait()
+    own = mm(pick, q_ref[...]).astype(BF)
+    for i in range(NA + NB):
+        qa[i, x, y, z] = own[0:16, i * HD : (i + 1) * HD]
+        qb[i, y, x, z] = own[16:32, i * HD : (i + 1) * HD]
+    loads[2].wait()
 
     pl.semaphore_wait(barrier, len(peers))
 
     cz = copies(lambda d: (cnt.at[x, y, z],) * 2, zp, Z)
-    az = copies(lambda d: (qa.at[x, y, z],) * 2, zp, Z)
-    bz = copies(lambda d: (qb.at[y, x, z],) * 2, zp, Z)
+    az = copies(lambda d: (qa.at[:, x, y, z],) * 2, zp, Z)
+    bz = copies(lambda d: (qb.at[:, y, x, z],) * 2, zp, Z)
     start(cz)
     start(az)
     start(bz)
@@ -162,74 +189,70 @@
     sel[...] = onehot(((lane & 7) == (col >> log2(HD))) & (lane < 24))
     ht[...] = jnp.zeros_like(ht)
 
+    groups = [pl.ds(0, NA), pl.ds(NA, NB)]
     cy = copies(lambda d: (cnt.at[x, y],) * 2, yp, Y)
-    ay = copies(lambda d: (qa.at[x, y],) * 2, yp, Y)
-    bx = copies(lambda d: (qb.at[y, x],) * 2, xp, X)
+    ay = [copies(lambda d: (qa.at[g, x, y],) * 2, yp, Y) for g in groups]
+    bx = [copies(lambda d: (qb.at[g, y, x],) * 2, xp, X) for g in groups]
+    cx = copies(lambda d: (cnt.at[x],) * 2, xp, X)
+    ax = [ring(lambda i, lo, hi: qa.at[g, i, :, pl.ds(lo, hi - lo)], xp, X, x) for g in groups]
+    by = [ring(lambda i, lo, hi: qb.at[g, i, :, pl.ds(lo, hi - lo)], yp, Y, y) for g in groups]
     arrive(cz)
     start(cy)
     arrive(az)
-    start(ay)
+    start(ay[0])
     arrive(bz)
-    start(bx)
-    cx = copies(lambda d: (cnt.at[x],) * 2, xp, X)
-    ax = copies(lambda d: (qa.at[x],) * 2, xp, X)
-    by = copies(lambda d: (qb.at[y],) * 2, yp, Y)
+    start(bx[0])
+    start(ay[1])
+    start(bx[1])
+    loads[4].wait()
+    for i in range(NA + NB):
+        vx[i, :, :HD] = v_ref[:, i * HD : (i + 1) * HD]
+        vx[i, :, HD:] = jnp.ones((tok, HD), BF)
+    loads[3].wait()
     arrive(cy)
     start(cx)
-    arrive(ay)
-    start(ax)
-    arrive(bx)
-    start(by)
+    arrive(ay[0])
+    start(ax[0][0])
+    arrive(bx[0])
+    start(by[0][0])
+    arrive(ay[1])
+    start(ax[1][0])
+    arrive(bx[1])
+    start(by[1][0])
     arrive(cx)
 
     counts = jnp.sum(cnt[...].reshape(X * Y * Z, HD), axis=0, keepdims=True)
     cnt8 = jnp.broadcast_to(counts, (8, HD)).astype(BF)
-
-    def positions(part, block, size):
+    size = X * Y * Z * 16
+
+    def positions(part):
         j = iota((HD, size), 1)
         zz = (j >> 4) & (Z - 1)
-        o = j >> (4 + log2(Z))
-        s = ((o * X + block) if part == 0 else (block * X + o)) * Z + zz
+        i = j >> (4 + log2(Z))
+        if part == 0:
+            s = ((i & (Y - 1)) * X + (i >> log2(Y))) * Z + zz
+        else:
+            s = j >> 4
         b = iota((HD, size), 0)
         off = mm(cnt8, onehot(b < s))[0:1, :]
         n = mm(cnt8, onehot(b == s))[0:1, :]
         r = ((j[0:1, :] & 15) + 16 * part).astype(F32)
         return jnp.where(r < n, off + r, -1.0)
 
-    def compact(part, block, size, rows, first):
-        pos = positions(part, block, size)
-
-        @pl.loop(0, Y)
-        def _(yb):
-            i = iota((X * CR, size), 0) + yb * (X * CR)
-            got = mm(onehot(i.astype(F32) == pos), rows).astype(BF)
-            qc[yb] = got if first else qc[yb] + got
-
-    compact(0, x, bs_a, qa[x].reshape(bs_a, feat), True)
-    compact(1, y, bs_b, qb[y].reshape(bs_b, feat), False)
+    pos_a, pos_b = positions(0), positions(1)
+
+    @pl.loop(0, Y)
+    def _(yb):
+        i = (iota((X * CR, size), 0) + yb * (X * CR)).astype(F32)
+        pma[yb] = onehot(i == pos_a)
+        pmb[yb] = onehot(i == pos_b)
+
     slot, b = iota((Z * CAP, HD), 0), iota((Z * CAP, HD), 1)
     off = mm_nt(onehot(b < (y * X + x) * Z + (slot >> log2(CAP))), cnt8)[:, 0:1]
     want = off + (slot[:, 0:1] & (CAP - 1)).astype(F32)
     rsel[...] = onehot(iota((Z * CAP, nr), 1).astype(F32) == want)
 
-    for d in range(1, max(X, Y)):
-        if d < X:
-            arrive(ax[d - 1 : d])
-            xb = (x - d) & (X - 1)
-            compact(0, xb, bs_a, qa[xb].reshape(bs_a, feat), False)
-        if d < Y:
-            arrive(by[d - 1 : d])
-            yb = (y - d) & (Y - 1)
-            compact(1, yb, bs_b, qb[yb].reshape(bs_b, feat), False)
-
-    wy0 = copies(lambda d: (wt.at[y, :, :, w0],) * 2, yp, Y)
-    wx1 = copies(lambda d: (wt.at[:, x, :, w1],) * 2, xp, X)
-    arrive(wx0)
-    start(wy0)
-    arrive(wy1)
-    start(wx1)
-
-    scale = 1.0 / HD**0.5
+    scale = 1.0 / (HD**0.5 * math.log(2.0))
 
     def attend(first, heads, dest):
         @pl.loop(0, Y)
@@ -238,22 +261,39 @@
             tile = jnp.zeros((X * CR, HD), F32)
             for i in range(heads):
                 c = slice((first + i) * HD, (first + i + 1) * HD)
-                score = mm_nt(qc[yb, :, c], k_ref[:, c]) * scale
+                rows = mm(pma[yb], qa[first + i].reshape(size, HD)) + mm(pmb[yb], qb[first + i].reshape(size, HD))
+                score = mm_nt(rows.astype(BF), k_ref[:, c]) * scale
                 peak = jnp.max(score, axis=1, keepdims=True)
-                expo = jnp.exp(score - peak)
-                total = jnp.sum(expo, axis=1, keepdims=True)
-                part = mm(expo.astype(BF), v_ref[:, c]) / total
-                dest[yb, :, :, i * HD : (i + 1) * HD] = part.astype(BF).reshape(X, CR, HD)
-                tile = jnp.where((lane & 7) == i, peak + jnp.log(total), tile)
+                expo = lax.exp2(score - peak).astype(BF)
+                both = mm(expo, vx[first + i])
+                total = both[:, HD:]
+                dest[yb, :, :, i * HD : (i + 1) * HD] = (both[:, :HD] / total).astype(BF).reshape(X, CR, HD)
+                tile = jnp.where((lane & 7) == i, peak + log2_of(total), tile)
             dest[yb, :, :, heads * HD :] = pack_stat(tile).reshape(X, CR, HD)
 
+    arrive(ax[0][0])
+    start(ax[0][1])
+    arrive(by[0][0])
+    start(by[0][1])
+    arrive(ax[0][1])
+    arrive(by[0][1])
     attend(0, NA, pa)
     sa = copies(lambda d: (pa.at[(y + d) & (Y - 1)], ra.at[d - 1]), yp, Y)
     start(sa)
+    arrive(ax[1][0])
+    start(ax[1][1])
+    arrive(by[1][0])
+    start(by[1][1])
+    arrive(ax[1][1])
+    arrive(by[1][1])
     attend(NA, NB, pb)
     sb = copies(lambda d: (pb.at[:, (x + d) & (X - 1)], rb.at[d - 1]), xp, X)
     start(sb)
 
+    arrive(wx0)
+    arrive(wy1)
+    wy0 = copies(lambda d: (wt.at[y, :, :, w0],) * 2, yp, Y)
+    wx1 = copies(lambda d: (wt.at[:, x, :, w1],) * 2, xp, X)
     arrive(sa)
 
     @pl.loop(0, X)
@@ -264,6 +304,7 @@
 
     sa2 = copies(lambda d: (a2.at[(x + d) & (X - 1)], ra2.at[d - 1]), xp, X)
     start(sa2)
+    start(wy0)
     arrive(sb)
 
     @pl.loop(0, Y)
@@ -274,6 +315,7 @@
 
     sb2 = copies(lambda d: (b2.at[(y + d) & (Y - 1)], rb2.at[d - 1]), yp, Y)
     start(sb2)
+    start(wx1)
     arrive(sa2)
     mean, logs = merge([a2[x]] + [ra2[d] for d in range(X - 1)], NA, sel[...])
     a3[:, :half] = mean.astype(BF)
@@ -307,12 +349,19 @@
         proj = proj + hr[d - 1].astype(F32)
     fin[y, x] = proj.astype(BF)
 
-    fx = copies(lambda d: (fin.at[y, x],) * 2, xp, X)
-    start(fx)
-    arrive(fx)
-    fy = copies(lambda d: (fin.at[y],) * 2, yp, Y)
-    start(fy)
-    arrive(fy)
+    f0, f1 = pl.ds(0, HD), pl.ds(HD, HD)
+    fx0 = copies(lambda d: (fin.at[y, x, :, f0],) * 2, xp, X)
+    fy1 = copies(lambda d: (fin.at[y, x, :, f1],) * 2, yp, Y)
+    start(fx0)
+    start(fy1)
+    fy0 = copies(lambda d: (fin.at[y, :, :, f0],) * 2, yp, Y)
+    fx1 = copies(lambda d: (fin.at[:, x, :, f1],) * 2, xp, X)
+    arrive(fx0)
+    start(fy0)
+    arrive(fy1)
+    start(fx1)
+    arrive(fy0)
+    arrive(fx1)
     zs[...] = mm(rsel[...], fin[...].reshape(nr, 2 * HD)).astype(BF).reshape(Z, CAP, 2 * HD)
     sz = copies(lambda d: (zs.at[(z + d) & (Z - 1)], zr.at[d - 1]), zp, Z)
     start(sz)
@@ -327,6 +376,8 @@
     for d in range(1, Z):
         arrive(sz[d - 1 : d])
         rows = rows + place(zr[d - 1], (z - d) & (Z - 1))
+    loads[5].wait()
+    loads[6].wait()
     grown = mm(expand[...], rows.astype(BF))
     live = mm(expand[...], jnp.ones((CAP, feat), BF)) > 0.5
     out_ref[...] = jnp.where(live, hid_ref[...].astype(F32) + grown, cac_ref[...].astype(F32)).astype(BF)
@@ -337,26 +388,35 @@
 def shards(queries, keys, values, hidden, cached, active, w_out):
     tok, feat = queries.shape
     wc = w_out.shape[1]
+    size = X * Y * Z * 16
     wa, wb = (NA + 1) * HD, (NB + 1) * HD
-    n_copies = 3 * (Z - 1) + 5 * (X - 1) + 5 * (Y - 1) + 2 * (X + Y - 2) + 3 * (Z - 1) + (H - 1) + 3 * (X + Y)
+    n_copies = 160
     vmem = pltpu.VMEM
     scratch = [
-        vmem((X, Y, Z, 16, feat), BF),
-        vmem((Y, X, Z, 16, feat), BF),
+        vmem((tok, feat), BF),
+        vmem((tok, feat), BF),
+        vmem((tok, feat), BF),
+        vmem((tok, feat), BF),
+        vmem((tok, feat), BF),
+        vmem((1, tok), jnp.int32),
+        vmem((NA + NB, X, Y, Z, 16, HD), BF),
+        vmem((NA + NB, Y, X, Z, 16, HD), BF),
         vmem((X, Y, Z, 1, HD), F32),
         vmem((Y, X, wc, feat), BF),
-        vmem((Y, X * CR, feat), BF),
+        vmem((Y, X * CR, size), BF),
+        vmem((Y, X * CR, size), BF),
+        vmem((NA + NB, tok, 2 * HD), BF),
         vmem((HD, NA * HD), BF),
         vmem((Z * CAP, Y * X * CR), BF),
         vmem((tok, CAP), BF),
         vmem((Y, X, CR, wa), BF),
         vmem((Y, X, CR, wb), BF),
-        vmem((Y - 1, X, CR, wa), BF),
-        vmem((X - 1, Y, CR, wb), BF),
+        vmem((max(Y - 1, 1), X, CR, wa), BF),
+        vmem((max(X - 1, 1), Y, CR, wb), BF),
         vmem((X, CR, wa), BF),
         vmem((Y, CR, wb), BF),
-        vmem((X - 1, CR, wa), BF),
-        vmem((Y - 1, CR, wb), BF),
+        vmem((max(X - 1, 1), CR, wa), BF),
+        vmem((max(Y - 1, 1), CR, wb), BF),
         vmem((CR, wa), BF),
         vmem((CR, wb), BF),
         vmem((Z - 1, CR, wa), BF),
@@ -368,17 +428,18 @@
         vmem((Z - 1, CAP, 2 * HD), BF),
         pltpu.SemaphoreType.DMA((n_copies,)),
         pltpu.SemaphoreType.DMA((n_copies,)),
+        pltpu.SemaphoreType.DMA((7,)),
     ]
     return pl.pallas_call(
         body,
         out_shape=jax.ShapeDtypeStruct((tok, feat), BF),
-        in_specs=[pl.BlockSpec(memory_space=pltpu.VMEM)] * 7,
+        in_specs=[pl.BlockSpec(memory_space=pl.ANY)] * 7,
         out_specs=pl.BlockSpec(memory_space=pltpu.VMEM),
         scratch_shapes=scratch,
         compiler_params=pltpu.CompilerParams(
-            collective_id=0, has_side_effects=True, vmem_limit_bytes=48 * 2**20
+            collective_id=0, has_side_effects=True, vmem_limit_bytes=60 * 2**20
         ),
-    )(queries, keys, values, hidden, cached, active.reshape(1, tok), w_out)
+    )(queries, keys, values, hidden, cached, active.reshape(1, tok), w_out.T)
 
 
 def solution(mesh):

time: 113 us -> 108 us (0.956)
  local copies, waits for them, and re-layouts: 6.66 us -> 1.73 us
    unnamed x14 -> x1, local copies, waits for them, and re-layouts: 6.66 us -> 1.73 us
where the time goes in v2:
time: 108 us
  Pallas kernels  107 us (99%)
  local copies, waits for them, and re-layouts  1.73 us (2%)
    pallas_call x1, Pallas kernels, shards(): pl.pallas_call(body, out_shape=jax.ShapeDtypeStruct((tok, feat), BF), in_...  107 us

profile of v2, /device:TPU:1, one launch (start us, length us, event | category | flops | bytes accessed | tf_op | source)
XLA Modules:
  0.0 108.3 jit_solution(10762472184189077234)
XLA Ops:
  0.0 106.5 %shard_map.73 = bf16[256,640]{1,0:T(8,128)(2,1)} custom-call(bf16[256,640]{1,0:T(8,128)(2,1)} %q_hbm.1, bf16[256,640]{1,0:T(8,128)(2,1)} %k_hbm.1, bf16[256,640]{1,0:T(8,128)(2,1)} %v_hbm.1, bf16[256,640]{1,0:T(8,128)(2,1)} %hid_hbm.1, bf16[256,640]{1,0:T(8,128)(2,1)} %cac_hbm.1, s32[1,256]{1,0:T(1,128)} %bitcast.3, bf16[80,640]{1,0:T(8,128)(2,1)} %bitcast.2), custom_call_target="tpu_custom_call" | custom-call | tf_op jit(solution)/shard_map/pallas_call | solution.py:433
  106.6 1.7 %copy.9 = bf16[256,640]{1,0:T(8,128)(2,1)} copy(bf16[256,640]{1,0:T(8,128)(2,1)} %shard_map.73) | data formatting | bytes 655360

commit v3 on v1

v3 whole, which is shorter than its diff:
```python
import math

import jax
import jax.numpy as jnp
from jax import lax
from jax.experimental import pallas as pl
from jax.experimental.pallas import tpu as pltpu
from jax.sharding import PartitionSpec as P

X, Y, Z, H = 4, 4, 4, 8
HD = 128
CAP = 32
BF = jnp.bfloat16
F32 = jnp.float32
NA, NB = 3, 2
MESH = pl.DeviceIdType.MESH


def log2(n):
    return n.bit_length() - 1


def iota(shape, dim):
    return lax.broadcasted_iota(jnp.int32, shape, dim)


def onehot(cond):
    return jnp.where(cond, 1.0, 0.0).astype(BF)


def log2_of(v):
    return jnp.log(v) * (1.0 / math.log(2.0))


def mm(a, b):
    return jnp.dot(a, b, preferred_element_type=F32)


def mm_nt(a, b):
    return lax.dot_general(a, b, (((1,), (1,)), ((), ())), preferred_element_type=F32)


def pack_stat(tile):
    lane = iota(tile.shape, 1)
    hi = tile.astype(BF).astype(F32)
    rest = tile - hi
    mid = rest.astype(BF).astype(F32)
    low = rest - mid
    return jnp.where(lane < 8, hi, jnp.where(lane < 16, mid, jnp.where(lane < 24, low, 0.0))).astype(BF)


def merge(sources, heads, sel):
    width = heads * HD
    logs = [mm(s[:, width:], sel[:, :width]) for s in sources]
    top = logs[0]
    for part in logs[1:]:
        top = jnp.maximum(top, part)
    total, mixed = None, None
    for s, part in zip(sources, logs):
        w = lax.exp2(part - top)
        term = w * s[:, :width].astype(F32)
        total = w if total is None else total + w
        mixed = term if mixed is None else mixed + term
    return mixed / total, top + log2_of(total)


def stat_of(logs, heads):
    lane = iota((logs.shape[0], HD), 1)
    tile = jnp.zeros((logs.shape[0], HD), F32)
    for h in range(heads):
        tile = jnp.where((lane & 7) == h, logs[:, h * HD : (h + 1) * HD], tile)
    return pack_stat(tile)


def body(
    q_hbm, k_hbm, v_hbm, hid_hbm, cac_hbm, act_hbm, w_hbm, out_ref,
    q_ref, hid_ref, cac_ref, act_ref,
    ka, va, kb, vb, qa, qb, wt, sel, expand,
    sum_a, peak_a, sum_b, peak_b,
    pa, pb, ra, rb, a2, b2, ra2, rb2, at,
    ht, hr, zs, zr, send_sem, recv_sem, load_sem,
):
    tok, feat = q_ref.shape
    wc = w_hbm.shape[0]
    half = NA * HD
    me, h = lax.axis_index("seq"), lax.axis_index("head")
    z = me & (Z - 1)
    x = (me >> log2(Z)) & (X - 1)
    y = me >> log2(Z * X)

    def xp(d):
        return (y * X + ((x + d) & (X - 1))) * Z + z, h

    def yp(d):
        return (((y + d) & (Y - 1)) * X + x) * Z + z, h

    def zp(d):
        return (y * X + x) * Z + ((z + d) & (Z - 1)), h

    def hp(d):
        return me, (h + d) & (H - 1)

    barrier = pltpu.get_barrier_semaphore()
    peers = (
        [xp(d) for d in range(1, X)] + [yp(d) for d in range(1, Y)] + [zp(d) for d in range(1, Z)] + [hp(d) for d in range(1, H)]
    )
    for p in peers:
        pl.semaphore_signal(barrier, inc=1, device_id=p, device_id_type=MESH)

    lo, hi = pl.ds(0, half), pl.ds(half, feat - half)
    loads = [
        pltpu.make_async_copy(src, dst, load_sem.at[i])
        for i, (src, dst) in enumerate(
            [
                (act_hbm, act_ref), (q_hbm, q_ref),
                (k_hbm.at[:, lo], ka.at[x]), (k_hbm.at[:, hi], kb.at[y]),
                (v_hbm.at[:, lo], va.at[x]), (v_hbm.at[:, hi], vb.at[y]),
                (w_hbm, wt.at[y, x]), (hid_hbm, hid_ref), (cac_hbm, cac_ref),
            ]
        )
    ]
    for c in loads:
        c.start()

    counter = [0]
    every = []

    def copies(make, peer, steps):
        found = []
        for d in steps:
            i = counter[0]
            counter[0] += 1
            src, dst = make(d)
            found.append(
                pltpu.make_async_remote_copy(
                    src_ref=src, dst_ref=dst, send_sem=send_sem.at[i], recv_sem=recv_sem.at[i],
                    device_id=peer(d), device_id_type=MESH,
                )
            )
        return found

    def start(cs):
        for c in cs:
            c.start()
        every.extend(cs)

    def arrive(cs):
        for c in cs:
            c.wait_recv()

    def near(n):
        return [1, n - 1] if n > 2 else list(range(1, n))

    def far(n):
        return list(range(2, n - 1))

    every_x, every_y, every_z, every_h = range(1, X), range(1, Y), range(1, Z), range(1, H)

    loads[0].wait()
    act = act_ref[...]
    act8 = jnp.broadcast_to(act, (8, tok)).astype(F32).astype(BF)
    before = onehot(iota((tok, tok), 0) < iota((tok, tok), 1))
    rank = mm(act8, before)[0:1, :]
    pick = onehot((iota((CAP, tok), 0).astype(F32) == rank) & (act > 0))
    loads[1].wait()
    own = mm(pick, q_ref[...]).astype(BF)
    qa[y, z] = own[:, :half]
    qb[x, z] = own[:, half:]
    for c in loads[2:7]:
        c.wait()

    pl.semaphore_wait(barrier, len(peers))

    az = copies(lambda d: (qa.at[y, z],) * 2, zp, every_z)
    bz = copies(lambda d: (qb.at[x, z],) * 2, zp, every_z)
    start(az)
    start(bz)
    ka1 = copies(lambda d: (ka.at[x],) * 2, xp, near(X)) + copies(lambda d: (va.at[x],) * 2, xp, near(X))
    kb1 = copies(lambda d: (kb.at[y],) * 2, yp, near(Y)) + copies(lambda d: (vb.at[y],) * 2, yp, near(Y))
    ka2 = copies(lambda d: (ka.at[x],) * 2, xp, far(X)) + copies(lambda d: (va.at[x],) * 2, xp, far(X))
    kb2 = copies(lambda d: (kb.at[y],) * 2, yp, far(Y)) + copies(lambda d: (vb.at[y],) * 2, yp, far(Y))
    start(ka1)
    start(kb1)

    expand[...] = mm_nt(onehot(iota((tok, tok), 0) == iota((tok, tok), 1)), pick).astype(BF)
    lane, col = iota((HD, half), 0), iota((HD, half), 1)
    sel[...] = onehot(((lane & 7) == (col >> log2(HD))) & (lane < 24))

    ay = copies(lambda d: (qa.at[y],) * 2, yp, every_y)
    bx = copies(lambda d: (qb.at[x],) * 2, xp, every_x)
    arrive(az)
    start(ay)
    arrive(bz)
    start(bx)
    start(ka2)
    start(kb2)

    wx0 = copies(lambda d: (wt.at[y, x, :, lo],) * 2, xp, every_x)
    wy1 = copies(lambda d: (wt.at[y, x, :, hi],) * 2, yp, every_y)
    wy0 = copies(lambda d: (wt.at[y, :, :, lo],) * 2, yp, every_y)
    wx1 = copies(lambda d: (wt.at[:, x, :, hi],) * 2, xp, every_x)
    start(wx0)
    start(wy1)

    scale = 1.0 / (HD**0.5 * math.log(2.0))
    ones = jnp.ones((tok, HD), BF)
    group = Z * CAP

    def attend(heads, rows, k, v, blocks, sums, peaks, dest, first, last):
        @pl.loop(0, rows.shape[0])
        def _(g):
            lane = iota((group, HD), 1)
            tile = jnp.zeros((group, HD), F32)
            for i in range(heads):
                c = slice(i * HD, (i + 1) * HD)
                query = rows[g, :, :, c].reshape(group, HD)
                scores = [mm_nt(query, k[b, :, c]) * scale for b in blocks]
                peak = jnp.max(scores[0], axis=1, keepdims=True)
                for score in scores[1:]:
                    peak = jnp.maximum(peak, jnp.max(score, axis=1, keepdims=True))
                if not first:
                    old = peaks[g, i]
                    peak = jnp.maximum(old, peak)
                both = None
                for b, score in zip(blocks, scores):
                    expo = lax.exp2(score - peak[:, 0:1]).astype(BF)
                    part = mm(expo, jnp.concatenate([v[b, :, c], ones], axis=1))
                    both = part if both is None else both + part
                if not first:
                    fade = lax.exp2(old - peak)
                    both = both + sums[g, i] * jnp.concatenate([fade, fade], axis=1)
                if last:
                    total = both[:, HD:]
                    dest[g, :, :, c] = (both[:, :HD] / total).astype(BF).reshape(Z, CAP, HD)
                    tile = jnp.where((lane & 7) == i, peak + log2_of(total), tile)
                else:
                    sums[g, i] = both
                    peaks[g, i] = jnp.broadcast_to(peak, (group, HD))
            if last:
                dest[g, :, :, heads * HD :] = pack_stat(tile).reshape(Z, CAP, HD)

    def near_blocks(at_, n):
        return [at_] + [(at_ - d) & (n - 1) for d in near(n)]

    def far_blocks(at_, n):
        return [(at_ - d) & (n - 1) for d in far(n)]

    arrive(ay)
    arrive(ka1)
    attend(NA, qa, ka, va, near_blocks(x, X), sum_a, peak_a, pa, True, X <= 3)
    arrive(bx)
    arrive(kb1)
    attend(NB, qb, kb, vb, near_blocks(y, Y), sum_b, peak_b, pb, True, Y <= 3)
    arrive(ka2)
    if X > 3:
        attend(NA, qa, ka, va, far_blocks(x, X), sum_a, peak_a, pa, False, True)
    sa = copies(lambda d: (pa.at[(y + d) & (Y - 1)], ra.at[d - 1]), yp, every_y)
    start(sa)
    arrive(kb2)
    if Y > 3:
        attend(NB, qb, kb, vb, far_blocks(y, Y), sum_b, peak_b, pb, False, True)
    sb = copies(lambda d: (pb.at[(x + d) & (X - 1)], rb.at[d - 1]), xp, every_x)
    start(sb)
    arrive(wx0)
    arrive(wy1)
    start(wy0)
    start(wx1)

    arrive(sa)

    @pl.loop(0, Z)
    def _(i):
        mean, logs = merge([pa[y, i]] + [ra[d, i] for d in range(Y - 1)], NA, sel[...])
        a2[i, :, :half] = mean.astype(BF)
        a2[i, :, half:] = stat_of(logs, NA)

    sa2 = copies(lambda d: (a2.at[(z + d) & (Z - 1)], ra2.at[d - 1]), zp, every_z)
    start(sa2)
    arrive(sb)

    @pl.loop(0, Z)
    def _(i):
        mean, logs = merge([pb[x, i]] + [rb[d, i] for d in range(X - 1)], NB, sel[...])
        b2[i, :, : NB * HD] = mean.astype(BF)
        b2[i, :, NB * HD :] = stat_of(logs, NB)

    sb2 = copies(lambda d: (b2.at[(z + d) & (Z - 1)], rb2.at[d - 1]), zp, every_z)
    start(sb2)
    arrive(sa2)
    at[z, :, :half] = merge([a2[z]] + [ra2[d] for d in range(Z - 1)], NA, sel[...])[0].astype(BF)
    arrive(sb2)
    at[z, :, half:] = merge([b2[z]] + [rb2[d] for d in range(Z - 1)], NB, sel[...])[0].astype(BF)
    tz = copies(lambda d: (at.at[z],) * 2, zp, every_z)
    start(tz)
    arrive(tz)
    arrive(wy0)
    arrive(wx1)

    pieces = X * Y // H
    extra = pieces * wc - HD
    attn = at[...].reshape(group, feat)
    for o in range(H):
        yy, xx = o * pieces // X, o * pieces % X
        term = mm_nt(attn, wt[yy, xx : xx + pieces].reshape(pieces * wc, feat))
        ht[o, 0:group] = term[:, :HD].astype(BF)
        for i in range(Z):
            ht[o, group:, i * extra : (i + 1) * extra] = term[i * CAP : (i + 1) * CAP, HD:].astype(BF)
    sh = copies(lambda d: (ht.at[(h + d) & (H - 1)], hr.at[d - 1]), hp, every_h)
    start(sh)
    proj = ht[h].astype(F32)
    for d in every_h:
        arrive(sh[d - 1 : d])
        proj = proj + hr[d - 1].astype(F32)
    lane = iota((CAP, HD), 1)
    for i in range(Z):
        zs[i, 0:CAP] = proj[i * CAP : (i + 1) * CAP].astype(BF)
        zs[i, CAP:] = jnp.where((lane >= i * extra) & (lane < (i + 1) * extra), proj[group:], 0.0).astype(BF)

    sz = copies(lambda d: (zs.at[(z + d) & (Z - 1)], zr.at[d - 1]), zp, every_z)
    start(sz)

    def place(rows, zz):
        l, c = iota((HD, feat), 0), iota((HD, feat), 1)
        p1 = l
        p2 = HD + l - z * extra
        t1 = jnp.where(p1 >= wc, (Z - 1) * wc, 0) + zz * wc + p1
        t2 = jnp.where(p2 >= wc, (Z - 1) * wc, 0) + zz * wc + p2
        inside = (l >= z * extra) & (l < (z + 1) * extra)
        return mm(rows[0:CAP], onehot(c == t1)) + mm(rows[CAP:], onehot((c == t2) & inside))

    rows = place(zs[z], z)
    for d in every_z:
        arrive(sz[d - 1 : d])
        rows = rows + place(zr[d - 1], (z - d) & (Z - 1))
    loads[7].wait()
    loads[8].wait()
    grown = mm(expand[...], rows.astype(BF))
    live = mm(expand[...], jnp.ones((CAP, feat), BF)) > 0.5
    out_ref[...] = jnp.where(live, hid_ref[...].astype(F32) + grown, cac_ref[...].astype(F32)).astype(BF)
    for c in every:
        c.wait_send()


def shards(queries, keys, values, hidden, cached, active, w_out):
    tok, feat = queries.shape
    wc = w_out.shape[1]
    fa, fb = NA * HD, NB * HD
    wa, wb = fa + HD, fb + HD
    group = Z * CAP
    n_copies = 120
    vmem = pltpu.VMEM
    scratch = [
        vmem((tok, feat), BF),
        vmem((tok, feat), BF),
        vmem((tok, feat), BF),
        vmem((1, tok), jnp.int32),
        vmem((X, tok, fa), BF),
        vmem((X, tok, fa), BF),
        vmem((Y, tok, fb), BF),
        vmem((Y, tok, fb), BF),
        vmem((Y, Z, CAP, fa), BF),
        vmem((X, Z, CAP, fb), BF),
        vmem((Y, X, wc, feat), BF),
        vmem((HD, fa), BF),
        vmem((tok, CAP), BF),
        vmem((Y, NA, group, 2 * HD), F32),
        vmem((Y, NA, group, HD), F32),
        vmem((X, NB, group, 2 * HD), F32),
        vmem((X, NB, group, HD), F32),
        vmem((Y, Z, CAP, wa), BF),
        vmem((X, Z, CAP, wb), BF),
        vmem((max(Y - 1, 1), Z, CAP, wa), BF),
        vmem((max(X - 1, 1), Z, CAP, wb), BF),
        vmem((Z, CAP, wa), BF),
        vmem((Z, CAP, wb), BF),
        vmem((Z - 1, CAP, wa), BF),
        vmem((Z - 1, CAP, wb), BF),
        vmem((Z, CAP, feat), BF),
        vmem((H, group + CAP, HD), BF),
        vmem((H - 1, group + CAP, HD), BF),
        vmem((Z, 2 * CAP, HD), BF),
        vmem((Z - 1, 2 * CAP, HD), BF),
        pltpu.SemaphoreType.DMA((n_copies,)),
        pltpu.SemaphoreType.DMA((n_copies,)),
        pltpu.SemaphoreType.DMA((9,)),
    ]
    return pl.pallas_call(
        body,
        out_shape=jax.ShapeDtypeStruct((tok, feat), BF),
        in_specs=[pl.BlockSpec(memory_space=pl.ANY)] * 7,
        out_specs=pl.BlockSpec(memory_space=pltpu.VMEM),
        scratch_shapes=scratch,
        compiler_params=pltpu.CompilerParams(
            collective_id=0, has_side_effects=True, vmem_limit_bytes=60 * 2**20
        ),
    )(queries, keys, values, hidden, cached, active.reshape(1, tok), w_out.T)


def solution(mesh):
    placed = (
        P("seq", "head"),
        P("seq", "head"),
        P("seq", "head"),
        P("seq", "head"),
        P("seq", "head"),
        P("seq"),
        P("head", "seq"),
    )
    return jax.shard_map(
        shards, mesh=mesh, in_specs=placed, out_specs=P("seq", "head"), check_vma=False
    )
```

time: 113 us -> 88.2 us (0.78)
  Pallas kernels: 106 us -> 86.3 us
  local copies, waits for them, and re-layouts: 6.66 us -> 1.73 us
    pallas_call x1, Pallas kernels: 106 us -> 86.3 us  [shards(): pl.pallas_call(body, out_shape=jax.ShapeDtypeStruct((tok, feat), BF), in_...]
    unnamed x14 -> x1, local copies, waits for them, and re-layouts: 6.66 us -> 1.73 us
where the time goes in v3:
time: 88.2 us; the launch traced here: 88.1 us
  Pallas kernels  86.3 us (98%)
  local copies, waits for them, and re-layouts  1.73 us (2%)
    pallas_call x1, Pallas kernels, shards(): pl.pallas_call(body, out_shape=jax.ShapeDtypeStruct((tok, feat), BF), in_...  86.3 us

profile of v3, /device:TPU:1, one launch (start us, length us, event | category | flops | bytes accessed | tf_op | source)
XLA Modules:
  0.0 88.1 jit_solution(2180883064125916943)
XLA Ops:
  0.0 86.3 %shard_map.73 = bf16[256,640]{1,0:T(8,128)(2,1)} custom-call(bf16[256,640]{1,0:T(8,128)(2,1)} %q_hbm.1, bf16[256,640]{1,0:T(8,128)(2,1)} %k_hbm.1, bf16[256,640]{1,0:T(8,128)(2,1)} %v_hbm.1, bf16[256,640]{1,0:T(8,128)(2,1)} %hid_hbm.1, bf16[256,640]{1,0:T(8,128)(2,1)} %cac_hbm.1, s32[1,256]{1,0:T(1,128)} %bitcast.3, bf16[80,640]{1,0:T(8,128)(2,1)} %bitcast.2), custom_call_target="tpu_custom_call" | custom-call | tf_op jit(solution)/shard_map/pallas_call | solution.py:387
  86.4 1.7 %copy.9 = bf16[256,640]{1,0:T(8,128)(2,1)} copy(bf16[256,640]{1,0:T(8,128)(2,1)} %shard_map.73) | data formatting | bytes 655360

commit v4 on v3

--- a/solution.py
+++ b/solution.py
@@ -78,7 +78,7 @@
     ka, va, kb, vb, qa, qb, wt, sel, expand,
     sum_a, peak_a, sum_b, peak_b,
     pa, pb, ra, rb, a2, b2, ra2, rb2, at,
-    ht, hr, zs, zr, send_sem, recv_sem, load_sem,
+    ht, hc, hs, hr, zs, zr, send_sem, recv_sem, load_sem,
 ):
     tok, feat = q_ref.shape
     wc = w_hbm.shape[0]
@@ -97,12 +97,15 @@
     def zp(d):
         return (y * X + x) * Z + ((z + d) & (Z - 1)), h
 
+    def cp(d):
+        return me, h ^ 1
+
     def hp(d):
-        return me, (h + d) & (H - 1)
+        return me, (((h >> 1) + d) & (H // 2 - 1)) * 2 + (h & 1)
 
     barrier = pltpu.get_barrier_semaphore()
     peers = (
-        [xp(d) for d in range(1, X)] + [yp(d) for d in range(1, Y)] + [zp(d) for d in range(1, Z)] + [hp(d) for d in range(1, H)]
+        [xp(d) for d in range(1, X)] + [yp(d) for d in range(1, Y)] + [zp(d) for d in range(1, Z)] + [hp(d) for d in range(1, H // 2)] + [cp(1)]
     )
     for p in peers:
         pl.semaphore_signal(barrier, inc=1, device_id=p, device_id_type=MESH)
@@ -154,7 +157,24 @@
     def far(n):
         return list(range(2, n - 1))
 
-    every_x, every_y, every_z, every_h = range(1, X), range(1, Y), range(1, Z), range(1, H)
+    def relay(block, peer, n, at_):
+        if n <= 3:
+            return []
+        on = copies(lambda d: (block((at_ - 1) & (n - 1), 0),) * 2, peer, [1])
+        return on + copies(lambda d: (block((at_ + 1) & (n - 1), 1),) * 2, peer, [n - 1])
+
+    every_x, every_y, every_z, every_h = range(1, X), range(1, Y), range(1, Z), range(1, H // 2)
+
+    pl.semaphore_wait(barrier, len(peers))
+
+    ka1 = copies(lambda d: (k_hbm.at[:, lo], ka.at[x]), xp, near(X))
+    va1 = copies(lambda d: (v_hbm.at[:, lo], va.at[x]), xp, near(X))
+    kb1 = copies(lambda d: (k_hbm.at[:, hi], kb.at[y]), yp, near(Y))
+    vb1 = copies(lambda d: (v_hbm.at[:, hi], vb.at[y]), yp, near(Y))
+    start(ka1)
+    start(kb1)
+    start(va1)
+    start(vb1)
 
     loads[0].wait()
     act = act_ref[...]
@@ -166,41 +186,43 @@
     own = mm(pick, q_ref[...]).astype(BF)
     qa[y, z] = own[:, :half]
     qb[x, z] = own[:, half:]
-    for c in loads[2:7]:
-        c.wait()
-
-    pl.semaphore_wait(barrier, len(peers))
-
     az = copies(lambda d: (qa.at[y, z],) * 2, zp, every_z)
     bz = copies(lambda d: (qb.at[x, z],) * 2, zp, every_z)
     start(az)
     start(bz)
-    ka1 = copies(lambda d: (ka.at[x],) * 2, xp, near(X)) + copies(lambda d: (va.at[x],) * 2, xp, near(X))
-    kb1 = copies(lambda d: (kb.at[y],) * 2, yp, near(Y)) + copies(lambda d: (vb.at[y],) * 2, yp, near(Y))
-    ka2 = copies(lambda d: (ka.at[x],) * 2, xp, far(X)) + copies(lambda d: (va.at[x],) * 2, xp, far(X))
-    kb2 = copies(lambda d: (kb.at[y],) * 2, yp, far(Y)) + copies(lambda d: (vb.at[y],) * 2, yp, far(Y))
-    start(ka1)
-    start(kb1)
 
     expand[...] = mm_nt(onehot(iota((tok, tok), 0) == iota((tok, tok), 1)), pick).astype(BF)
     lane, col = iota((HD, half), 0), iota((HD, half), 1)
     sel[...] = onehot(((lane & 7) == (col >> log2(HD))) & (lane < 24))
 
+    for c in loads[2:7]:
+        c.wait()
     ay = copies(lambda d: (qa.at[y],) * 2, yp, every_y)
     bx = copies(lambda d: (qb.at[x],) * 2, xp, every_x)
+    ka2 = relay(lambda i, part: ka.at[i, pl.ds(part * (tok // 2), tok // 2)], xp, X, x)
+    va2 = relay(lambda i, part: va.at[i, pl.ds(part * (tok // 2), tok // 2)], xp, X, x)
+    kb2 = relay(lambda i, part: kb.at[i, pl.ds(part * (tok // 2), tok // 2)], yp, Y, y)
+    vb2 = relay(lambda i, part: vb.at[i, pl.ds(part * (tok // 2), tok // 2)], yp, Y, y)
     arrive(az)
     start(ay)
     arrive(bz)
     start(bx)
+    arrive(kb1)
+    start(kb2)
+    arrive(ka1)
     start(ka2)
-    start(kb2)
-
-    wx0 = copies(lambda d: (wt.at[y, x, :, lo],) * 2, xp, every_x)
-    wy1 = copies(lambda d: (wt.at[y, x, :, hi],) * 2, yp, every_y)
-    wy0 = copies(lambda d: (wt.at[y, :, :, lo],) * 2, yp, every_y)
-    wx1 = copies(lambda d: (wt.at[:, x, :, hi],) * 2, xp, every_x)
-    start(wx0)
-    start(wy1)
+    arrive(vb1)
+    start(vb2)
+    arrive(va1)
+    start(va2)
+
+    cut = [pl.ds(0, 48), pl.ds(48, wc - 48)]
+    wy0 = copies(lambda d: (wt.at[y, x, :, lo],) * 2, yp, every_y)
+    wx1 = copies(lambda d: (wt.at[y, x, :, hi],) * 2, xp, every_x)
+    wx0 = copies(lambda d: (wt.at[:, x, :, lo],) * 2, xp, near(X))
+    wy1 = copies(lambda d: (wt.at[y, :, :, hi],) * 2, yp, near(Y))
+    wx0 = [wx0, relay(lambda i, part: wt.at[:, i, cut[part], lo], xp, X, x)]
+    wy1 = [wy1, relay(lambda i, part: wt.at[i, :, cut[part], hi], yp, Y, y)]
 
     scale = 1.0 / (HD**0.5 * math.log(2.0))
     ones = jnp.ones((tok, HD), BF)
@@ -246,25 +268,27 @@
         return [(at_ - d) & (n - 1) for d in far(n)]
 
     arrive(ay)
-    arrive(ka1)
     attend(NA, qa, ka, va, near_blocks(x, X), sum_a, peak_a, pa, True, X <= 3)
     arrive(bx)
-    arrive(kb1)
     attend(NB, qb, kb, vb, near_blocks(y, Y), sum_b, peak_b, pb, True, Y <= 3)
+    start(wy0)
+    start(wx1)
     arrive(ka2)
+    arrive(va2)
     if X > 3:
         attend(NA, qa, ka, va, far_blocks(x, X), sum_a, peak_a, pa, False, True)
     sa = copies(lambda d: (pa.at[(y + d) & (Y - 1)], ra.at[d - 1]), yp, every_y)
     start(sa)
     arrive(kb2)
+    arrive(vb2)
     if Y > 3:
         attend(NB, qb, kb, vb, far_blocks(y, Y), sum_b, peak_b, pb, False, True)
     sb = copies(lambda d: (pb.at[(x + d) & (X - 1)], rb.at[d - 1]), xp, every_x)
     start(sb)
-    arrive(wx0)
-    arrive(wy1)
-    start(wy0)
-    start(wx1)
+    arrive(wy0)
+    arrive(wx1)
+    start(wx0[0])
+    start(wy1[0])
 
     arrive(sa)
 
@@ -286,6 +310,10 @@
 
     sb2 = copies(lambda d: (b2.at[(z + d) & (Z - 1)], rb2.at[d - 1]), zp, every_z)
     start(sb2)
+    arrive(wx0[0])
+    start(wx0[1])
+    arrive(wy1[0])
+    start(wy1[1])
     arrive(sa2)
     at[z, :, :half] = merge([a2[z]] + [ra2[d] for d in range(Z - 1)], NA, sel[...])[0].astype(BF)
     arrive(sb2)
@@ -293,8 +321,8 @@
     tz = copies(lambda d: (at.at[z],) * 2, zp, every_z)
     start(tz)
     arrive(tz)
-    arrive(wy0)
-    arrive(wx1)
+    arrive(wx0[1])
+    arrive(wy1[1])
 
     pieces = X * Y // H
     extra = pieces * wc - HD
@@ -302,12 +330,16 @@
     for o in range(H):
         yy, xx = o * pieces // X, o * pieces % X
         term = mm_nt(attn, wt[yy, xx : xx + pieces].reshape(pieces * wc, feat))
-        ht[o, 0:group] = term[:, :HD].astype(BF)
+        ht[o & 1, o >> 1, 0:group] = term[:, :HD].astype(BF)
         for i in range(Z):
-            ht[o, group:, i * extra : (i + 1) * extra] = term[i * CAP : (i + 1) * CAP, HD:].astype(BF)
-    sh = copies(lambda d: (ht.at[(h + d) & (H - 1)], hr.at[d - 1]), hp, every_h)
+            ht[o & 1, o >> 1, group:, i * extra : (i + 1) * extra] = term[i * CAP : (i + 1) * CAP, HD:].astype(BF)
+    sc = copies(lambda d: (ht.at[1 - (h & 1)], hc), cp, [1])
+    start(sc)
+    arrive(sc)
+    hs[...] = (ht[h & 1].astype(F32) + hc[...].astype(F32)).astype(BF)
+    sh = copies(lambda d: (hs.at[((h >> 1) + d) & (H // 2 - 1)], hr.at[d - 1]), hp, every_h)
     start(sh)
-    proj = ht[h].astype(F32)
+    proj = hs[h >> 1].astype(F32)
     for d in every_h:
         arrive(sh[d - 1 : d])
         proj = proj + hr[d - 1].astype(F32)
@@ -376,8 +408,10 @@
         vmem((Z - 1, CAP, wa), BF),
         vmem((Z - 1, CAP, wb), BF),
         vmem((Z, CAP, feat), BF),
-        vmem((H, group + CAP, HD), BF),
-        vmem((H - 1, group + CAP, HD), BF),
+        vmem((2, H // 2, group + CAP, HD), BF),
+        vmem((H // 2, group + CAP, HD), BF),
+        vmem((H // 2, group + CAP, HD), BF),
+        vmem((max(H // 2 - 1, 1), group + CAP, HD), BF),
         vmem((Z, 2 * CAP, HD), BF),
         vmem((Z - 1, 2 * CAP, HD), BF),
         pltpu.SemaphoreType.DMA((n_copies,)),

time: 88.2 us -> 79.3 us (0.90)
  Pallas kernels: 86.3 us -> 77.4 us
    pallas_call x1, Pallas kernels: 86.3 us -> 77.4 us  [shards(): pl.pallas_call(body, out_shape=jax.ShapeDtypeStruct((tok, feat), BF), in_...]
where the time goes in v4:
time: 79.3 us; the launch traced here: 79.1 us
  Pallas kernels  77.4 us (98%)
  local copies, waits for them, and re-layouts  1.73 us (2%)
    pallas_call x1, Pallas kernels, shards(): pl.pallas_call(body, out_shape=jax.ShapeDtypeStruct((tok, feat), BF), in_...  77.4 us
    unnamed x1, local copies, waits for them, and re-layouts  1.73 us

profile of v4, /device:TPU:1, one launch (start us, length us, event | category | flops | bytes accessed | tf_op | source)
XLA Modules:
  0.0 79.1 jit_solution(14652248353083174312)
XLA Ops:
  0.0 77.4 %shard_map.73 = bf16[256,640]{1,0:T(8,128)(2,1)} custom-call(bf16[256,640]{1,0:T(8,128)(2,1)} %q_hbm.1, bf16[256,640]{1,0:T(8,128)(2,1)} %k_hbm.1, bf16[256,640]{1,0:T(8,128)(2,1)} %v_hbm.1, bf16[256,640]{1,0:T(8,128)(2,1)} %hid_hbm.1, bf16[256,640]{1,0:T(8,128)(2,1)} %cac_hbm.1, s32[1,256]{1,0:T(1,128)} %bitcast.3, bf16[80,640]{1,0:T(8,128)(2,1)} %bitcast.2), custom_call_target="tpu_custom_call" | custom-call | tf_op jit(solution)/shard_map/pallas_call | solution.py:421
  77.4 1.7 %copy.9 = bf16[256,640]{1,0:T(8,128)(2,1)} copy(bf16[256,640]{1,0:T(8,128)(2,1)} %shard_map.73) | data formatting | bytes 655360

commit v5 on v4

--- a/solution.py
+++ b/solution.py
@@ -78,7 +78,7 @@
     ka, va, kb, vb, qa, qb, wt, sel, expand,
     sum_a, peak_a, sum_b, peak_b,
     pa, pb, ra, rb, a2, b2, ra2, rb2, at,
-    ht, hc, hs, hr, zs, zr, send_sem, recv_sem, load_sem,
+    ht, hc, hs, hr, zs, zr, base, places, send_sem, recv_sem, load_sem,
 ):
     tok, feat = q_ref.shape
     wc = w_hbm.shape[0]
@@ -167,14 +167,25 @@
 
     pl.semaphore_wait(barrier, len(peers))
 
-    ka1 = copies(lambda d: (k_hbm.at[:, lo], ka.at[x]), xp, near(X))
-    va1 = copies(lambda d: (v_hbm.at[:, lo], va.at[x]), xp, near(X))
-    kb1 = copies(lambda d: (k_hbm.at[:, hi], kb.at[y]), yp, near(Y))
-    vb1 = copies(lambda d: (v_hbm.at[:, hi], vb.at[y]), yp, near(Y))
-    start(ka1)
-    start(kb1)
-    start(va1)
-    start(vb1)
+    parts = [pl.ds(0, tok // 2), pl.ds(tok // 2, tok // 2)]
+
+    def near_copies(src, cols, dst, at_, peer, n, second):
+        found = []
+        for d in near(n):
+            rows = parts[int(d != 1) ^ second]
+            found += copies(lambda _: (src.at[rows, cols], dst.at[at_, rows]), peer, [d])
+        return found
+
+    ka1, va1, kb1, vb1 = ([
+        near_copies(src, cols, dst, at_, peer, n, second) for second in (0, 1)
+    ] for src, cols, dst, at_, peer, n in (
+        (k_hbm, lo, ka, x, xp, X), (v_hbm, lo, va, x, xp, X), (k_hbm, hi, kb, y, yp, Y), (v_hbm, hi, vb, y, yp, Y),
+    ))
+    for i in range(2):
+        start(ka1[i])
+        start(kb1[i])
+        start(va1[i])
+        start(vb1[i])
 
     loads[0].wait()
     act = act_ref[...]
@@ -195,26 +206,38 @@
     lane, col = iota((HD, half), 0), iota((HD, half), 1)
     sel[...] = onehot(((lane & 7) == (col >> log2(HD))) & (lane < 24))
 
-    for c in loads[2:7]:
+    for c in loads[2:]:
         c.wait()
+    live = mm(expand[...], jnp.ones((CAP, feat), BF)) > 0.5
+    base[...] = jnp.where(live, hid_ref[...].astype(F32), cac_ref[...].astype(F32)).astype(BF)
+    pieces = X * Y // H
+    extra = pieces * wc - HD
+    l, c = iota((2 * HD, feat), 0), iota((2 * HD, feat), 1)
+    piece = jnp.where(l < HD, l, l - z * extra)
+    mine = (l < HD) | ((l >= HD + z * extra) & (l < HD + (z + 1) * extra))
+    goal = jnp.where(piece >= wc, (Z - 1) * wc, 0) + piece
+    for d in range(Z):
+        places[d] = onehot((goal + ((z - d) & (Z - 1)) * wc == c) & mine)
     ay = copies(lambda d: (qa.at[y],) * 2, yp, every_y)
     bx = copies(lambda d: (qb.at[x],) * 2, xp, every_x)
-    ka2 = relay(lambda i, part: ka.at[i, pl.ds(part * (tok // 2), tok // 2)], xp, X, x)
-    va2 = relay(lambda i, part: va.at[i, pl.ds(part * (tok // 2), tok // 2)], xp, X, x)
-    kb2 = relay(lambda i, part: kb.at[i, pl.ds(part * (tok // 2), tok // 2)], yp, Y, y)
-    vb2 = relay(lambda i, part: vb.at[i, pl.ds(part * (tok // 2), tok // 2)], yp, Y, y)
+    ka2 = relay(lambda i, part: ka.at[i, parts[part]], xp, X, x)
+    va2 = relay(lambda i, part: va.at[i, parts[part]], xp, X, x)
+    kb2 = relay(lambda i, part: kb.at[i, parts[part]], yp, Y, y)
+    vb2 = relay(lambda i, part: vb.at[i, parts[part]], yp, Y, y)
     arrive(az)
     start(ay)
     arrive(bz)
     start(bx)
-    arrive(kb1)
+    arrive(ka1[0])
+    start(ka2)
+    arrive(kb1[0])
     start(kb2)
-    arrive(ka1)
-    start(ka2)
-    arrive(vb1)
+    arrive(va1[0])
+    start(va2)
+    arrive(vb1[0])
     start(vb2)
-    arrive(va1)
-    start(va2)
+    arrive(ka1[1])
+    arrive(va1[1])
 
     cut = [pl.ds(0, 48), pl.ds(48, wc - 48)]
     wy0 = copies(lambda d: (wt.at[y, x, :, lo],) * 2, yp, every_y)
@@ -270,9 +293,9 @@
     arrive(ay)
     attend(NA, qa, ka, va, near_blocks(x, X), sum_a, peak_a, pa, True, X <= 3)
     arrive(bx)
+    arrive(kb1[1])
+    arrive(vb1[1])
     attend(NB, qb, kb, vb, near_blocks(y, Y), sum_b, peak_b, pb, True, Y <= 3)
-    start(wy0)
-    start(wx1)
     arrive(ka2)
     arrive(va2)
     if X > 3:
@@ -285,10 +308,8 @@
         attend(NB, qb, kb, vb, far_blocks(y, Y), sum_b, peak_b, pb, False, True)
     sb = copies(lambda d: (pb.at[(x + d) & (X - 1)], rb.at[d - 1]), xp, every_x)
     start(sb)
-    arrive(wy0)
-    arrive(wx1)
-    start(wx0[0])
-    start(wy1[0])
+    start(wy0)
+    start(wx1)
 
     arrive(sa)
 
@@ -300,6 +321,8 @@
 
     sa2 = copies(lambda d: (a2.at[(z + d) & (Z - 1)], ra2.at[d - 1]), zp, every_z)
     start(sa2)
+    arrive(wx1)
+    start(wy1[0])
     arrive(sb)
 
     @pl.loop(0, Z)
@@ -310,22 +333,22 @@
 
     sb2 = copies(lambda d: (b2.at[(z + d) & (Z - 1)], rb2.at[d - 1]), zp, every_z)
     start(sb2)
-    arrive(wx0[0])
-    start(wx0[1])
-    arrive(wy1[0])
-    start(wy1[1])
+    arrive(wy0)
+    start(wx0[0])
     arrive(sa2)
     at[z, :, :half] = merge([a2[z]] + [ra2[d] for d in range(Z - 1)], NA, sel[...])[0].astype(BF)
     arrive(sb2)
     at[z, :, half:] = merge([b2[z]] + [rb2[d] for d in range(Z - 1)], NB, sel[...])[0].astype(BF)
     tz = copies(lambda d: (at.at[z],) * 2, zp, every_z)
     start(tz)
+    arrive(wy1[0])
+    start(wy1[1])
+    arrive(wx0[0])
+    start(wx0[1])
     arrive(tz)
     arrive(wx0[1])
     arrive(wy1[1])
 
-    pieces = X * Y // H
-    extra = pieces * wc - HD
     attn = at[...].reshape(group, feat)
     for o in range(H):
         yy, xx = o * pieces // X, o * pieces % X
@@ -345,30 +368,17 @@
         proj = proj + hr[d - 1].astype(F32)
     lane = iota((CAP, HD), 1)
     for i in range(Z):
-        zs[i, 0:CAP] = proj[i * CAP : (i + 1) * CAP].astype(BF)
-        zs[i, CAP:] = jnp.where((lane >= i * extra) & (lane < (i + 1) * extra), proj[group:], 0.0).astype(BF)
+        zs[i, :, :HD] = proj[i * CAP : (i + 1) * CAP].astype(BF)
+        zs[i, :, HD:] = jnp.where((lane >= i * extra) & (lane < (i + 1) * extra), proj[group:], 0.0).astype(BF)
 
     sz = copies(lambda d: (zs.at[(z + d) & (Z - 1)], zr.at[d - 1]), zp, every_z)
     start(sz)
 
-    def place(rows, zz):
-        l, c = iota((HD, feat), 0), iota((HD, feat), 1)
-        p1 = l
-        p2 = HD + l - z * extra
-        t1 = jnp.where(p1 >= wc, (Z - 1) * wc, 0) + zz * wc + p1
-        t2 = jnp.where(p2 >= wc, (Z - 1) * wc, 0) + zz * wc + p2
-        inside = (l >= z * extra) & (l < (z + 1) * extra)
-        return mm(rows[0:CAP], onehot(c == t1)) + mm(rows[CAP:], onehot((c == t2) & inside))
-
-    rows = place(zs[z], z)
+    rows = mm(zs[z], places[0])
     for d in every_z:
         arrive(sz[d - 1 : d])
-        rows = rows + place(zr[d - 1], (z - d) & (Z - 1))
-    loads[7].wait()
-    loads[8].wait()
-    grown = mm(expand[...], rows.astype(BF))
-    live = mm(expand[...], jnp.ones((CAP, feat), BF)) > 0.5
-    out_ref[...] = jnp.where(live, hid_ref[...].astype(F32) + grown, cac_ref[...].astype(F32)).astype(BF)
+        rows = rows + mm(zr[d - 1], places[d])
+    out_ref[...] = (base[...].astype(F32) + mm(expand[...], rows.astype(BF))).astype(BF)
     for c in every:
         c.wait_send()
 
@@ -412,8 +422,10 @@
         vmem((H // 2, group + CAP, HD), BF),
         vmem((H // 2, group + CAP, HD), BF),
         vmem((max(H // 2 - 1, 1), group + CAP, HD), BF),
-        vmem((Z, 2 * CAP, HD), BF),
-        vmem((Z - 1, 2 * CAP, HD), BF),
+        vmem((Z, CAP, 2 * HD), BF),
+        vmem((Z - 1, CAP, 2 * HD), BF),
+        vmem((tok, feat), BF),
+        vmem((Z, 2 * HD, feat), BF),
         pltpu.SemaphoreType.DMA((n_copies,)),
         pltpu.SemaphoreType.DMA((n_copies,)),
         pltpu.SemaphoreType.DMA((9,)),

time: 79.3 us -> 80 us (level)
  no operation moved by 1% of the time
where the time goes in v5:
time: 80 us; the launch traced here: 79.9 us
  Pallas kernels  78.1 us (98%)
  local copies, waits for them, and re-layouts  1.73 us (2%)
    pallas_call x1, Pallas kernels, shards(): pl.pallas_call(body, out_shape=jax.ShapeDtypeStruct((tok, feat), BF), in_...  78.1 us
    unnamed x1, local copies, waits for them, and re-layouts  1.73 us

profile of v5, /device:TPU:1, one launch (start us, length us, event | category | flops | bytes accessed | tf_op | source)
XLA Modules:
  0.0 79.9 jit_solution(14960784649873439563)
XLA Ops:
  0.0 78.1 %shard_map.73 = bf16[256,640]{1,0:T(8,128)(2,1)} custom-call(bf16[256,640]{1,0:T(8,128)(2,1)} %q_hbm.1, bf16[256,640]{1,0:T(8,128)(2,1)} %k_hbm.1, bf16[256,640]{1,0:T(8,128)(2,1)} %v_hbm.1, bf16[256,640]{1,0:T(8,128)(2,1)} %hid_hbm.1, bf16[256,640]{1,0:T(8,128)(2,1)} %cac_hbm.1, s32[1,256]{1,0:T(1,128)} %bitcast.3, bf16[80,640]{1,0:T(8,128)(2,1)} %bitcast.2), custom_call_target="tpu_custom_call" | custom-call | tf_op jit(solution)/shard_map/pallas_call | solution.py:433
  78.1 1.7 %copy.9 = bf16[256,640]{1,0:T(8,128)(2,1)} copy(bf16[256,640]{1,0:T(8,128)(2,1)} %shard_map.73) | data formatting | bytes 655360

commit v6 on v5

--- a/solution.py
+++ b/solution.py
@@ -181,11 +181,8 @@
     ] for src, cols, dst, at_, peer, n in (
         (k_hbm, lo, ka, x, xp, X), (v_hbm, lo, va, x, xp, X), (k_hbm, hi, kb, y, yp, Y), (v_hbm, hi, vb, y, yp, Y),
     ))
-    for i in range(2):
-        start(ka1[i])
-        start(kb1[i])
-        start(va1[i])
-        start(vb1[i])
+    for c in (ka1[0], kb1[0], va1[0], vb1[0], ka1[1], kb1[1]):
+        start(c)
 
     loads[0].wait()
     act = act_ref[...]
@@ -208,16 +205,6 @@
 
     for c in loads[2:]:
         c.wait()
-    live = mm(expand[...], jnp.ones((CAP, feat), BF)) > 0.5
-    base[...] = jnp.where(live, hid_ref[...].astype(F32), cac_ref[...].astype(F32)).astype(BF)
-    pieces = X * Y // H
-    extra = pieces * wc - HD
-    l, c = iota((2 * HD, feat), 0), iota((2 * HD, feat), 1)
-    piece = jnp.where(l < HD, l, l - z * extra)
-    mine = (l < HD) | ((l >= HD + z * extra) & (l < HD + (z + 1) * extra))
-    goal = jnp.where(piece >= wc, (Z - 1) * wc, 0) + piece
-    for d in range(Z):
-        places[d] = onehot((goal + ((z - d) & (Z - 1)) * wc == c) & mine)
     ay = copies(lambda d: (qa.at[y],) * 2, yp, every_y)
     bx = copies(lambda d: (qb.at[x],) * 2, xp, every_x)
     ka2 = relay(lambda i, part: ka.at[i, parts[part]], xp, X, x)
@@ -228,6 +215,8 @@
     start(ay)
     arrive(bz)
     start(bx)
+    start(va1[1])
+    start(vb1[1])
     arrive(ka1[0])
     start(ka2)
     arrive(kb1[0])
@@ -252,37 +241,37 @@
     group = Z * CAP
 
     def attend(heads, rows, k, v, blocks, sums, peaks, dest, first, last):
-        @pl.loop(0, rows.shape[0])
-        def _(g):
-            lane = iota((group, HD), 1)
-            tile = jnp.zeros((group, HD), F32)
-            for i in range(heads):
-                c = slice(i * HD, (i + 1) * HD)
-                query = rows[g, :, :, c].reshape(group, HD)
-                scores = [mm_nt(query, k[b, :, c]) * scale for b in blocks]
-                peak = jnp.max(scores[0], axis=1, keepdims=True)
-                for score in scores[1:]:
-                    peak = jnp.maximum(peak, jnp.max(score, axis=1, keepdims=True))
-                if not first:
-                    old = peaks[g, i]
-                    peak = jnp.maximum(old, peak)
-                both = None
-                for b, score in zip(blocks, scores):
-                    expo = lax.exp2(score - peak[:, 0:1]).astype(BF)
-                    part = mm(expo, jnp.concatenate([v[b, :, c], ones], axis=1))
-                    both = part if both is None else both + part
-                if not first:
-                    fade = lax.exp2(old - peak)
-                    both = both + sums[g, i] * jnp.concatenate([fade, fade], axis=1)
-                if last:
-                    total = both[:, HD:]
-                    dest[g, :, :, c] = (both[:, :HD] / total).astype(BF).reshape(Z, CAP, HD)
-                    tile = jnp.where((lane & 7) == i, peak + log2_of(total), tile)
-                else:
-                    sums[g, i] = both
-                    peaks[g, i] = jnp.broadcast_to(peak, (group, HD))
+        lines = rows.shape[0]
+        plane = lines * group
+        lane = iota((plane, HD), 1)
+        tile = jnp.zeros((plane, HD), F32)
+        for i in range(heads):
+            c = slice(i * HD, (i + 1) * HD)
+            query = rows[:, :, :, c].reshape(plane, HD)
+            scores = [mm_nt(query, k[b, :, c]) * scale for b in blocks]
+            peak = jnp.max(scores[0], axis=1, keepdims=True)
+            for score in scores[1:]:
+                peak = jnp.maximum(peak, jnp.max(score, axis=1, keepdims=True))
+            if not first:
+                old = peaks[i]
+                peak = jnp.maximum(old, peak)
+            both = None
+            for b, score in zip(blocks, scores):
+                expo = lax.exp2(score - peak[:, 0:1]).astype(BF)
+                part = mm(expo, jnp.concatenate([v[b, :, c], ones], axis=1))
+                both = part if both is None else both + part
+            if not first:
+                fade = lax.exp2(old - peak)
+                both = both + sums[i] * jnp.concatenate([fade, fade], axis=1)
             if last:
-                dest[g, :, :, heads * HD :] = pack_stat(tile).reshape(Z, CAP, HD)
+                total = both[:, HD:]
+                dest[:, :, :, c] = (both[:, :HD] / total).astype(BF).reshape(lines, Z, CAP, HD)
+                tile = jnp.where((lane & 7) == i, peak + log2_of(total), tile)
+            else:
+                sums[i] = both
+                peaks[i] = jnp.broadcast_to(peak, (plane, HD))
+        if last:
+            dest[:, :, :, heads * HD :] = pack_stat(tile).reshape(lines, Z, CAP, HD)
 
     def near_blocks(at_, n):
         return [at_] + [(at_ - d) & (n - 1) for d in near(n)]
@@ -296,6 +285,8 @@
     arrive(kb1[1])
     arrive(vb1[1])
     attend(NB, qb, kb, vb, near_blocks(y, Y), sum_b, peak_b, pb, True, Y <= 3)
+    start(wy0)
+    start(wx1)
     arrive(ka2)
     arrive(va2)
     if X > 3:
@@ -308,43 +299,46 @@
         attend(NB, qb, kb, vb, far_blocks(y, Y), sum_b, peak_b, pb, False, True)
     sb = copies(lambda d: (pb.at[(x + d) & (X - 1)], rb.at[d - 1]), xp, every_x)
     start(sb)
-    start(wy0)
-    start(wx1)
+    live = mm(expand[...], jnp.ones((CAP, feat), BF)) > 0.5
+    base[...] = jnp.where(live, hid_ref[...].astype(F32), cac_ref[...].astype(F32)).astype(BF)
+    pieces = X * Y // H
+    extra = pieces * wc - HD
+    l, c = iota((2 * HD, feat), 0), iota((2 * HD, feat), 1)
+    piece = jnp.where(l < HD, l, l - z * extra)
+    mine = (l < HD) | ((l >= HD + z * extra) & (l < HD + (z + 1) * extra))
+    goal = jnp.where(piece >= wc, (Z - 1) * wc, 0) + piece
+    for d in range(Z):
+        places[d] = onehot((goal + ((z - d) & (Z - 1)) * wc == c) & mine)
+    arrive(wy0)
+    arrive(wx1)
+    start(wx0[0])
+    start(wy1[0])
 
     arrive(sa)
 
-    @pl.loop(0, Z)
-    def _(i):
-        mean, logs = merge([pa[y, i]] + [ra[d, i] for d in range(Y - 1)], NA, sel[...])
-        a2[i, :, :half] = mean.astype(BF)
-        a2[i, :, half:] = stat_of(logs, NA)
-
+    def merge_in(dest, sources, heads):
+        mean, logs = merge([r.reshape(group, r.shape[-1]) for r in sources], heads, sel[...])
+        dest[:, :, : heads * HD] = mean.astype(BF).reshape(Z, CAP, heads * HD)
+        dest[:, :, heads * HD :] = stat_of(logs, heads).reshape(Z, CAP, HD)
+
+    merge_in(a2, [pa[y]] + [ra[d] for d in range(Y - 1)], NA)
     sa2 = copies(lambda d: (a2.at[(z + d) & (Z - 1)], ra2.at[d - 1]), zp, every_z)
     start(sa2)
-    arrive(wx1)
-    start(wy1[0])
     arrive(sb)
 
-    @pl.loop(0, Z)
-    def _(i):
-        mean, logs = merge([pb[x, i]] + [rb[d, i] for d in range(X - 1)], NB, sel[...])
-        b2[i, :, : NB * HD] = mean.astype(BF)
-        b2[i, :, NB * HD :] = stat_of(logs, NB)
-
+    merge_in(b2, [pb[x]] + [rb[d] for d in range(X - 1)], NB)
     sb2 = copies(lambda d: (b2.at[(z + d) & (Z - 1)], rb2.at[d - 1]), zp, every_z)
     start(sb2)
-    arrive(wy0)
-    start(wx0[0])
+    arrive(wx0[0])
+    start(wx0[1])
+    arrive(wy1[0])
+    start(wy1[1])
     arrive(sa2)
     at[z, :, :half] = merge([a2[z]] + [ra2[d] for d in range(Z - 1)], NA, sel[...])[0].astype(BF)
     arrive(sb2)
     at[z, :, half:] = merge([b2[z]] + [rb2[d] for d in range(Z - 1)], NB, sel[...])[0].astype(BF)
     tz = copies(lambda d: (at.at[z],) * 2, zp, every_z)
     start(tz)
-    arrive(wy1[0])
-    start(wy1[1])
-    arrive(wx0[0])
-    start(wx0[1])
     arrive(tz)
     arrive(wx0[1])
     arrive(wy1[1])
@@ -405,10 +399,10 @@
         vmem((Y, X, wc, feat), BF),
         vmem((HD, fa), BF),
         vmem((tok, CAP), BF),
-        vmem((Y, NA, group, 2 * HD), F32),
-        vmem((Y, NA, group, HD), F32),
-        vmem((X, NB, group, 2 * HD), F32),
-        vmem((X, NB, group, HD), F32),
+        vmem((NA, Y * group, 2 * HD), F32),
+        vmem((NA, Y * group, HD), F32),
+        vmem((NB, X * group, 2 * HD), F32),
+        vmem((NB, X * group, HD), F32),
         vmem((Y, Z, CAP, wa), BF),
         vmem((X, Z, CAP, wb), BF),
         vmem((max(Y - 1, 1), Z, CAP, wa), BF),

time: 80 us -> 77.6 us (0.970)
  Pallas kernels: 78.1 us -> 75.7 us
    pallas_call x1, Pallas kernels: 78.1 us -> 75.7 us  [shards(): pl.pallas_call(body, out_shape=jax.ShapeDtypeStruct((tok, feat), BF), in_...]
where the time goes in v6:
time: 77.6 us; the launch traced here: 77.4 us
  Pallas kernels  75.7 us (98%)
  local copies, waits for them, and re-layouts  1.73 us (2%)
    pallas_call x1, Pallas kernels, shards(): pl.pallas_call(body, out_shape=jax.ShapeDtypeStruct((tok, feat), BF), in_...  75.7 us
    unnamed x1, local copies, waits for them, and re-layouts  1.73 us

profile of v6, /device:TPU:1, one launch (start us, length us, event | category | flops | bytes accessed | tf_op | source)
XLA Modules:
  0.0 77.4 jit_solution(172837054493363033)
XLA Ops:
  0.0 75.7 %shard_map.73 = bf16[256,640]{1,0:T(8,128)(2,1)} custom-call(bf16[256,640]{1,0:T(8,128)(2,1)} %q_hbm.1, bf16[256,640]{1,0:T(8,128)(2,1)} %k_hbm.1, bf16[256,640]{1,0:T(8,128)(2,1)} %v_hbm.1, bf16[256,640]{1,0:T(8,128)(2,1)} %hid_hbm.1, bf16[256,640]{1,0:T(8,128)(2,1)} %cac_hbm.1, s32[1,256]{1,0:T(1,128)} %bitcast.3, bf16[80,640]{1,0:T(8,128)(2,1)} %bitcast.2), custom_call_target="tpu_custom_call" | custom-call | tf_op jit(solution)/shard_map/pallas_call | solution.py:427
  75.7 1.7 %copy.9 = bf16[256,640]{1,0:T(8,128)(2,1)} copy(bf16[256,640]{1,0:T(8,128)(2,1)} %shard_map.73) | data formatting | bytes 655360

commit v7 on v6

--- a/solution.py
+++ b/solution.py
@@ -309,12 +309,10 @@
     goal = jnp.where(piece >= wc, (Z - 1) * wc, 0) + piece
     for d in range(Z):
         places[d] = onehot((goal + ((z - d) & (Z - 1)) * wc == c) & mine)
-    arrive(wy0)
+
+    arrive(sa)
     arrive(wx1)
-    start(wx0[0])
     start(wy1[0])
-
-    arrive(sa)
 
     def merge_in(dest, sources, heads):
         mean, logs = merge([r.reshape(group, r.shape[-1]) for r in sources], heads, sel[...])
@@ -325,40 +323,60 @@
     sa2 = copies(lambda d: (a2.at[(z + d) & (Z - 1)], ra2.at[d - 1]), zp, every_z)
     start(sa2)
     arrive(sb)
+    arrive(wy0)
+    start(wx0[0])
 
     merge_in(b2, [pb[x]] + [rb[d] for d in range(X - 1)], NB)
     sb2 = copies(lambda d: (b2.at[(z + d) & (Z - 1)], rb2.at[d - 1]), zp, every_z)
     start(sb2)
+    arrive(sa2)
+    at[z, :, :half] = merge([a2[z]] + [ra2[d] for d in range(Z - 1)], NA, sel[...])[0].astype(BF)
+    tza = copies(lambda d: (at.at[z, :, lo],) * 2, zp, every_z)
+    start(tza)
+    arrive(wy1[0])
+    start(wy1[1])
     arrive(wx0[0])
     start(wx0[1])
-    arrive(wy1[0])
-    start(wy1[1])
-    arrive(sa2)
-    at[z, :, :half] = merge([a2[z]] + [ra2[d] for d in range(Z - 1)], NA, sel[...])[0].astype(BF)
     arrive(sb2)
     at[z, :, half:] = merge([b2[z]] + [rb2[d] for d in range(Z - 1)], NB, sel[...])[0].astype(BF)
-    tz = copies(lambda d: (at.at[z],) * 2, zp, every_z)
-    start(tz)
-    arrive(tz)
+    tzb = copies(lambda d: (at.at[z, :, hi],) * 2, zp, every_z)
+    start(tzb)
+    arrive(tza)
     arrive(wx0[1])
     arrive(wy1[1])
+    arrive(tzb)
 
     attn = at[...].reshape(group, feat)
-    for o in range(H):
-        yy, xx = o * pieces // X, o * pieces % X
-        term = mm_nt(attn, wt[yy, xx : xx + pieces].reshape(pieces * wc, feat))
-        ht[o & 1, o >> 1, 0:group] = term[:, :HD].astype(BF)
+    row, core, chips = h >> 1, h & 1, H // 2
+
+    def terms(which, j):
+        at_ = (2 * j + which) * pieces
+        w_o = wt[at_ >> log2(X), pl.ds(at_ & (X - 1), pieces)].reshape(pieces * wc, feat)
+        term = mm_nt(attn, w_o)
+        ht[which, j, 0:group] = term[:, :HD].astype(BF)
         for i in range(Z):
-            ht[o & 1, o >> 1, group:, i * extra : (i + 1) * extra] = term[i * CAP : (i + 1) * CAP, HD:].astype(BF)
-    sc = copies(lambda d: (ht.at[1 - (h & 1)], hc), cp, [1])
-    start(sc)
-    arrive(sc)
-    hs[...] = (ht[h & 1].astype(F32) + hc[...].astype(F32)).astype(BF)
-    sh = copies(lambda d: (hs.at[((h >> 1) + d) & (H // 2 - 1)], hr.at[d - 1]), hp, every_h)
-    start(sh)
-    proj = hs[h >> 1].astype(F32)
+            ht[which, j, group:, i * extra : (i + 1) * extra] = term[i * CAP : (i + 1) * CAP, HD:].astype(BF)
+
+    order = [(row + d) & (chips - 1) for d in [*every_h, 0]]
+    sc = []
+    for j in order:
+        terms(1 - core, j)
+        sc.append(copies(lambda d: (ht.at[1 - core, j], hc.at[j]), cp, [1]))
+        start(sc[-1])
+    for j in order:
+        terms(core, j)
+    sh = []
+    for d, j, c in zip([*every_h, 0], order, sc):
+        arrive(c)
+        both = ht[core, j].astype(F32) + hc[j].astype(F32)
+        if d:
+            hs[j] = both.astype(BF)
+            sh.append(copies(lambda _: (hs.at[j], hr.at[d - 1]), hp, [d]))
+            start(sh[-1])
+        else:
+            proj = both
     for d in every_h:
-        arrive(sh[d - 1 : d])
+        arrive(sh[d - 1])
         proj = proj + hr[d - 1].astype(F32)
     lane = iota((CAP, HD), 1)
     for i in range(Z):

time: 77.6 us -> 76.9 us (level)
  Pallas kernels: 75.7 us -> 74.8 us
    pallas_call x1, Pallas kernels: 75.7 us -> 74.8 us  [shards(): pl.pallas_call(body, out_shape=jax.ShapeDtypeStruct((tok, feat), BF), in_...]
where the time goes in v7:
time: 76.9 us; the launch traced here: 76.6 us
  Pallas kernels  74.8 us (97%)
  local copies, waits for them, and re-layouts  1.73 us (2%)
    pallas_call x1, Pallas kernels, shards(): pl.pallas_call(body, out_shape=jax.ShapeDtypeStruct((tok, feat), BF), in_...  74.8 us
    unnamed x1, local copies, waits for them, and re-layouts  1.73 us

profile of v7, /device:TPU:1, one launch (start us, length us, event | category | flops | bytes accessed | tf_op | source)
XLA Modules:
  0.0 76.6 jit_solution(10596408660851443730)
XLA Ops:
  0.0 74.8 %shard_map.73 = bf16[256,640]{1,0:T(8,128)(2,1)} custom-call(bf16[256,640]{1,0:T(8,128)(2,1)} %q_hbm.1, bf16[256,640]{1,0:T(8,128)(2,1)} %k_hbm.1, bf16[256,640]{1,0:T(8,128)(2,1)} %v_hbm.1, bf16[256,640]{1,0:T(8,128)(2,1)} %hid_hbm.1, bf16[256,640]{1,0:T(8,128)(2,1)} %cac_hbm.1, s32[1,256]{1,0:T(1,128)} %bitcast.3, bf16[80,640]{1,0:T(8,128)(2,1)} %bitcast.2), custom_call_target="tpu_custom_call" | custom-call | tf_op jit(solution)/shard_map/pallas_call | solution.py:445
  74.9 1.7 %copy.9 = bf16[256,640]{1,0:T(8,128)(2,1)} copy(bf16[256,640]{1,0:T(8,128)(2,1)} %shard_map.73) | data formatting | bytes 655360

commit v8 on v7

--- a/solution.py
+++ b/solution.py
@@ -279,14 +279,14 @@
     def far_blocks(at_, n):
         return [(at_ - d) & (n - 1) for d in far(n)]
 
+    start(wy0)
+    start(wx1)
     arrive(ay)
     attend(NA, qa, ka, va, near_blocks(x, X), sum_a, peak_a, pa, True, X <= 3)
     arrive(bx)
     arrive(kb1[1])
     arrive(vb1[1])
     attend(NB, qb, kb, vb, near_blocks(y, Y), sum_b, peak_b, pb, True, Y <= 3)
-    start(wy0)
-    start(wx1)
     arrive(ka2)
     arrive(va2)
     if X > 3:

time: 76.9 us -> 76.6 us (level)
  no operation moved by 1% of the time
where the time goes in v8:
time: 76.6 us; the launch traced here: 76.5 us
  Pallas kernels  74.7 us (98%)
  local copies, waits for them, and re-layouts  1.73 us (2%)
    pallas_call x1, Pallas kernels, shards(): pl.pallas_call(body, out_shape=jax.ShapeDtypeStruct((tok, feat), BF), in_...  74.7 us
    unnamed x1, local copies, waits for them, and re-layouts  1.73 us

profile of v8, /device:TPU:1, one launch (start us, length us, event | category | flops | bytes accessed | tf_op | source)
XLA Modules:
  0.0 76.5 jit_solution(7051456135133449219)
XLA Ops:
  0.0 74.7 %shard_map.73 = bf16[256,640]{1,0:T(8,128)(2,1)} custom-call(bf16[256,640]{1,0:T(8,128)(2,1)} %q_hbm.1, bf16[256,640]{1,0:T(8,128)(2,1)} %k_hbm.1, bf16[256,640]{1,0:T(8,128)(2,1)} %v_hbm.1, bf16[256,640]{1,0:T(8,128)(2,1)} %hid_hbm.1, bf16[256,640]{1,0:T(8,128)(2,1)} %cac_hbm.1, s32[1,256]{1,0:T(1,128)} %bitcast.3, bf16[80,640]{1,0:T(8,128)(2,1)} %bitcast.2), custom_call_target="tpu_custom_call" | custom-call | tf_op jit(solution)/shard_map/pallas_call | solution.py:445
  74.7 1.7 %copy.9 = bf16[256,640]{1,0:T(8,128)(2,1)} copy(bf16[256,640]{1,0:T(8,128)(2,1)} %shard_map.73) | data formatting | bytes 655360

commit v9 on v8

--- a/solution.py
+++ b/solution.py
@@ -299,6 +299,10 @@
         attend(NB, qb, kb, vb, far_blocks(y, Y), sum_b, peak_b, pb, False, True)
     sb = copies(lambda d: (pb.at[(x + d) & (X - 1)], rb.at[d - 1]), xp, every_x)
     start(sb)
+    arrive(wx1)
+    start(wy1[0])
+    arrive(wy0)
+    start(wx0[0])
     live = mm(expand[...], jnp.ones((CAP, feat), BF)) > 0.5
     base[...] = jnp.where(live, hid_ref[...].astype(F32), cac_ref[...].astype(F32)).astype(BF)
     pieces = X * Y // H
@@ -311,8 +315,6 @@
         places[d] = onehot((goal + ((z - d) & (Z - 1)) * wc == c) & mine)
 
     arrive(sa)
-    arrive(wx1)
-    start(wy1[0])
 
     def merge_in(dest, sources, heads):
         mean, logs = merge([r.reshape(group, r.shape[-1]) for r in sources], heads, sel[...])
@@ -323,8 +325,6 @@
     sa2 = copies(lambda d: (a2.at[(z + d) & (Z - 1)], ra2.at[d - 1]), zp, every_z)
     start(sa2)
     arrive(sb)
-    arrive(wy0)
-    start(wx0[0])
 
     merge_in(b2, [pb[x]] + [rb[d] for d in range(X - 1)], NB)
     sb2 = copies(lambda d: (b2.at[(z + d) & (Z - 1)], rb2.at[d - 1]), zp, every_z)

time: 76.6 us -> 76.1 us (level)
  no operation moved by 1% of the time
where the time goes in v9:
time: 76.1 us; the launch traced here: 75.9 us
  Pallas kernels  74.2 us (98%)
  local copies, waits for them, and re-layouts  1.73 us (2%)
    pallas_call x1, Pallas kernels, shards(): pl.pallas_call(body, out_shape=jax.ShapeDtypeStruct((tok, feat), BF), in_...  74.2 us
    unnamed x1, local copies, waits for them, and re-layouts  1.73 us

profile of v9, /device:TPU:1, one launch (start us, length us, event | category | flops | bytes accessed | tf_op | source)
XLA Modules:
  0.0 75.9 jit_solution(8284600881765231084)
XLA Ops:
  0.0 74.2 %shard_map.73 = bf16[256,640]{1,0:T(8,128)(2,1)} custom-call(bf16[256,640]{1,0:T(8,128)(2,1)} %q_hbm.1, bf16[256,640]{1,0:T(8,128)(2,1)} %k_hbm.1, bf16[256,640]{1,0:T(8,128)(2,1)} %v_hbm.1, bf16[256,640]{1,0:T(8,128)(2,1)} %hid_hbm.1, bf16[256,640]{1,0:T(8,128)(2,1)} %cac_hbm.1, s32[1,256]{1,0:T(1,128)} %bitcast.3, bf16[80,640]{1,0:T(8,128)(2,1)} %bitcast.2), custom_call_target="tpu_custom_call" | custom-call | tf_op jit(solution)/shard_map/pallas_call | solution.py:445
  74.2 1.7 %copy.9 = bf16[256,640]{1,0:T(8,128)(2,1)} copy(bf16[256,640]{1,0:T(8,128)(2,1)} %shard_map.73) | data formatting | bytes 655360
